TPU v7x, 128 devices: a whole 4x4x4 slice. The times are simulated.
128 devices in a mesh: wave: 64 (over z, y, x_lo, core), lev: 2 (over x_hi).
Axes of the slice: x: 4 (x_hi: 2, x_lo: 2; x = x_hi * 2 + x_lo), y: 4, z: 4, core: 2. Of those that a mesh axis runs over, the one named last changes fastest.
Arguments:
- spectra: bfloat16 [25600, 6, 3072], P('wave', None, 'lev'), may hold values from -0.4375 to 0.4375
- legendre: bfloat16 [25600, 64, 128], P('wave'), may hold values from -0.15625 to 0.15625
- block_slot: int32 [25600], P('wave'), may hold values from 0 to 20, as said below
- wavenumber: int32 [1280], replicated, may hold values from 0 to 1279, as said below
- cycle_points: int32 [128], P('wave'), may hold values from 20 to 5136, as said below
- quad_weight: float32 [128], P('wave'), may hold values from 0.02 to 0.2
Outputs:
- spectral_tendency: bfloat16 [25600, 6, 3072], P('wave', None, 'lev')
- grid_fields: bfloat16 [128, 3, 246528], P('wave', None, 'lev')
Inputs may be any that keep to these rules, and one draw needn't show every extreme that they name: `wavenumber`: A permutation of 0 .. 1279; slots d * 20 to (d + 1) * 20 - 1 belong to index d of wave, and one index holds the wavenumbers 0 .. 19. `block_slot`: among the 400 entries of one index of wave, each local slot whose wavenumber is m appears exactly 20 - m // 64 times, in any order; the other entries are 20; on the index that holds wavenumbers 0 .. 19 there are none. `cycle_points`: each value is 4 j + 20 for a cycle index j from the pole; some cycle has 5136 points and some 20.
All inputs are finite; a program needn't handle non-finite values.
Results may differ from a plain program's by a relative error of at most 0.008.
Values may be sent and summed in bfloat16 or wider, within the bound.
No kernel may reach another device: no remote copies, remote signals or barrier semaphores. Data moves between devices by JAX's collectives and lax.ppermute only.
A program may use at most 320 MiB of HBM per device.

v0:
```python
import math

import jax
import jax.numpy as jnp
from jax import lax
from jax.sharding import PartitionSpec as P

MMAX = 1280
NLON = 5136


def fourier_tables(points, wavenumber, columns):
    phases = wavenumber[None, :] * columns[:, None] % points
    angles = phases.astype(jnp.float32) * (2.0 * math.pi / points.astype(jnp.float32))
    inside = (2 * wavenumber[None, :] < points) & (columns[:, None] < points)
    cosine = jnp.where(inside, jnp.cos(angles), 0.0)
    sine_part = jnp.where(inside, -jnp.sin(angles), 0.0)
    return (cosine, sine_part)


def inverse_table(points, wavenumber, columns):
    cosine, sine_part = fourier_tables(points, wavenumber, columns)
    factor = jnp.where(wavenumber == 0, 1.0, 2.0).astype(jnp.float32)[None, :]
    return jnp.concatenate([cosine * factor, sine_part * factor], axis=1).astype(jnp.bfloat16)


def forward_table(points, wavenumber, columns):
    cosine, sine_part = fourier_tables(points, wavenumber, columns)
    return jnp.concatenate([cosine, sine_part], axis=1).astype(jnp.bfloat16)


def grid_products(grid_values):
    values = grid_values.astype(jnp.float32)
    return jnp.stack(
        [
            values[:, 0] * values[:, 2],
            values[:, 1] * values[:, 2],
            0.5 * values[:, 2] * values[:, 2],
        ],
        axis=1,
    ).astype(jnp.bfloat16)


def local(spectra, legendre, block_slot, wavenumber, cycle_points, quad_weight):
    block_count = spectra.shape[0]
    degree_count = legendre.shape[1]
    lev_count = spectra.shape[2] // degree_count
    slot_count = MMAX // lax.axis_size("wave")
    cycle_count = cycle_points.shape[0]
    slot_ids = jnp.arange(slot_count, dtype=jnp.int32)
    spec_view = spectra.reshape(block_count, 6, lev_count, degree_count)
    products = jnp.einsum("knj,kcln->kjcl", legendre, spec_view, preferred_element_type=jnp.float32)
    onehot = (block_slot[:, None] == slot_ids[None, :]).astype(jnp.float32)
    fourier = jnp.einsum("ks,kjcl->sjcl", onehot, products, precision=lax.Precision.HIGHEST).astype(
        jnp.bfloat16
    )
    received = lax.all_to_all(fourier, "wave", split_axis=1, concat_axis=0, tiled=True)
    unpacked = received.reshape(MMAX, cycle_count, 2, 3, lev_count)
    stacked = jnp.transpose(unpacked, (2, 0, 1, 3, 4)).reshape(2 * MMAX, cycle_count, 3, lev_count)
    all_columns = jnp.arange(NLON, dtype=jnp.int32)
    tables = jax.vmap(lambda points: inverse_table(points, wavenumber, all_columns))(cycle_points)
    grid_local = jnp.einsum(
        "rpk,krfl->rfpl", tables, stacked, preferred_element_type=jnp.float32
    ).astype(jnp.bfloat16)
    grid_parts = lax.all_to_all(grid_local, "lev", split_axis=2, concat_axis=3, tiled=True)
    half = grid_parts.shape[2]
    levels_all = grid_parts.shape[3]
    grid_fields = grid_parts.reshape(cycle_count, 3, half * levels_all)
    flux_terms = grid_products(grid_parts)
    flux_back = lax.all_to_all(flux_terms, "lev", split_axis=3, concat_axis=2, tiled=True)
    forward = jax.vmap(lambda points: forward_table(points, wavenumber, all_columns))(cycle_points)
    fourier_sums = jnp.einsum(
        "rpk,rfpl->rkfl", forward, flux_back, preferred_element_type=jnp.float32
    )
    weighted = fourier_sums * quad_weight[:, None, None, None]
    weighted = weighted.reshape(cycle_count, 2, MMAX, 3, lev_count)
    packed = (
        jnp.transpose(weighted, (2, 0, 1, 3, 4))
        .reshape(MMAX, cycle_count, 6 * lev_count)
        .astype(jnp.bfloat16)
    )
    returned = lax.all_to_all(packed, "wave", split_axis=0, concat_axis=1, tiled=True)
    extended = jnp.concatenate(
        [returned, jnp.zeros((1,) + returned.shape[1:], jnp.bfloat16)], axis=0
    )
    selected = extended[block_slot].reshape(block_count, returned.shape[1], 6, lev_count)
    tendency = jnp.einsum("knj,kjcl->kcln", legendre, selected, preferred_element_type=jnp.float32)
    spectral_tendency = tendency.reshape(block_count, 6, lev_count * degree_count).astype(
        jnp.bfloat16
    )
    return (spectral_tendency, grid_fields)


def solution(mesh):
    placed = (P("wave", None, "lev"), P("wave", None, None), P("wave"), P(), P("wave"), P("wave"))
    return jax.shard_map(
        local,
        mesh=mesh,
        in_specs=placed,
        out_specs=(P("wave", None, "lev"), P("wave", None, "lev")),
        check_vma=False,
    )
```

profile of v0, /device:TPU:1, one launch (start us, length us, event | category | flops | bytes accessed | tf_op | source)
XLA Modules:
  0.0 1136.3 jit_solution(18107005528891082506)
XLA Ops:
  0.6 11.5 %copy.95 = bf16[400,6,1536]{0,2,1:T(8,128)(2,1)} copy(bf16[400,6,1536]{2,0,1:T(8,128)(2,1)} %param.8) | data formatting | bytes 14745600 | tf_op args[0]
  12.1 17.7 %copy.96 = bf16[400,6,24,64]{3,2,1,0:T(8,128)(2,1)} copy(bf16[400,6,24,64]{0,3,2,1:T(8,128)(2,1)} %bitcast.73) | data formatting | bytes 14745600 | tf_op jit(solution)/shard_map/reshape | solution.py:51
  29.9 17.6 %fusion.19 = f32[400,128,6,24]{1,3,2,0:T(8,128)} fusion(bf16[400,6,24,64]{3,2,1,0:T(8,128)(2,1)} %copy.96, bf16[400,64,128]{2,1,0:T(8,128)(2,1)} %param.9), kind=kOutput, calls=%fused_computation.31 | convolution fusion | flops 943718400 | bytes 43417600 | tf_op jit(solution)/shard_map/knj,kcln->kjcl/dot_general | solution.py:52
  47.5 24.5 %fusion.21 = bf16[20,128,6,24]{1,0,3,2:T(8,128)(2,1)S(1)} fusion(f32[400,128,6,24]{1,3,2,0:T(8,128)} %fusion.19, s32[400]{0:T(512)S(1)} %copy-done.1), kind=kOutput, calls=%fused_computation.37 | convolution fusion | flops 1769848576 | bytes 30230080 | tf_op jit(solution)/shard_map/ks,kjcl->sjcl/dot_general | solution.py:54
  72.0 4.3 copy.98
  76.3 8.5 reshape.111
  84.8 11.1 all-to-all-start
  95.9 11.6 %iota_multiply_fusion = s32[5136,1280]{1,0:T(8,128)} fusion(s32[1280]{0:T(1024)S(1)} %copy-done), kind=kLoop, calls=%fused_computation.26 | loop fusion | flops 6574080 | bytes 26301440 | tf_op jit(solution)/shard_map/vmap()/mul | solution.py:13
  107.7 737.7 %multiply_convert_fusion.1 = (bf16[2,5136,1280]{2,1,0:T(8,128)(2,1)}, bf16[2,5136,1280]{2,1,0:T(8,128)(2,1)}, bf16[2,5136,1280]{2,1,0:T(8,128)(2,1)}, bf16[2,5136,1280]{2,1,0:T(8,128)(2,1)}) fusion(s32[2]{0:T(128)S(1)} %compare_select_fusion.2, s32[5136,1280]{1,0:T(8,128)} %iota_multiply_fusion, f32[1280]{0:T(1024)S(1)} %compare_select_fusion, ...), kind=kLoop, calls=%fused_computation.18 | loop fusion | flops 249815040 | bytes 131499568 | tf_op jit(solution)/shard_map/convert.4
  845.5 7.6 reshape.112
  853.1 9.9 copy.99
  863.0 13.0 %copy.100 = bf16[64,20,2,6,24]{1,0,4,3,2:T(8,128)(2,1)} copy(bf16[64,20,2,6,24]{4,2,0,3,1:T(2,128)(2,1)} %bitcast.78) | data formatting | bytes 1474560 | tf_op jit(solution)/shard_map/all_to_all | solution.py:57
  876.1 9.1 reshape.92
  885.2 22.5 %fusion.17 = bf16[2,3,5136,24]{2,3,1,0:T(8,128)(2,1)S(1)} fusion(bf16[2560,2,3,24]{0,3,2,1:T(8,128)(2,1)S(1)} %bitcast.87, bf16[2,5136,1280]{2,1,0:T(8,128)(2,1)} %get-tuple-element.18, bf16[2,5136,1280]{2,1,0:T(8,128)(2,1)} %get-tuple-element.17), kind=kOutput, calls=%fused_computation.29 | convolution fusion | flops 3892594944 | bytes 54809088 | tf_op jit(solution)/shard_map/rpk,krfl->rfpl/dot_general | solution.py:62
  907.7 13.5 %copy.102 = bf16[2,3,5136,24]{3,0,1,2:T(2,128)(2,1)} copy(bf16[2,3,5136,24]{2,3,1,0:T(8,128)(2,1)S(1)} %fusion.17) | data formatting | bytes 2958336 | tf_op jit(solution)/shard_map/convert_element_type | solution.py:64
  921.2 12.9 %reshape.113 = bf16[2,2,184896]{2,1,0:T(2,128)(2,1)S(1)} reshape(bf16[5136,3,2,24]{3,2,1,0:T(2,128)(2,1)} %bitcast.74) | data formatting | bytes 2958336
  934.1 22.8 %all_to_all.66 = bf16[2,2,184896]{2,1,0:T(2,128)(2,1)S(1)} all-to-all(bf16[2,2,184896]{2,1,0:T(2,128)(2,1)S(1)} %reshape.113), channel_id=1, replica_groups=mesh['wave'=64,'lev'=2] {'lev'}, dimensions={0} | all-to-all | bytes 2958336 | tf_op jit(solution)/shard_map/all_to_all | solution.py:65
  956.8 13.2 %reshape.114 = bf16[5136,3,2,24]{3,2,1,0:T(2,128)(2,1)} reshape(bf16[2,2,184896]{2,1,0:T(2,128)(2,1)S(1)} %all_to_all.66) | data formatting | bytes 2958336
  970.1 17.1 %copy.104 = bf16[2,3,2,2568,24]{3,4,2,1,0:T(8,128)(2,1)S(1)} copy(bf16[2,3,2,2568,24]{4,0,1,3,2:T(2,128)(2,1)} %bitcast.75) | data formatting | bytes 2958336 | tf_op jit(solution)/shard_map/all_to_all | solution.py:65
  989.1 21.3 %all_to_all.67 = bf16[2,3,2568,48]{2,0,1,3:T(2,128)(2,1)S(1)} all-to-all(bf16[2,3,2568,48]{2,0,1,3:T(2,128)(2,1)S(1)} %copy.105), channel_id=1, replica_groups=mesh['wave'=64,'lev'=2] {'lev'}, dimensions={3} | all-to-all | bytes 2958336 | tf_op jit(solution)/shard_map/all_to_all | solution.py:70
  1011.8 2.0 all_to_all.57
  1013.8 19.7 %fusion.5 = f32[2,2560,72]{1,2,0:S(1)} fusion(bf16[2,5136,72]{1,2,0:T(8,128)(2,1)} %bitcast.85, bf16[2,5136,1280]{2,1,0:T(8,128)(2,1)} %get-tuple-element.20, bf16[2,5136,1280]{2,1,0:T(8,128)(2,1)} %get-tuple-element.19), kind=kOutput, calls=%fused_computation.12 | convolution fusion | flops 3891855360 | bytes 55546368
  1033.7 2.7 copy.109
  1036.4 11.1 all-to-all-start.3
  1047.5 14.2 %copy.113 = bf16[2,3,2568,2,24]{4,3,2,0,1:T(2,128)(2,1)} copy(bf16[2,3,2568,2,24]{2,4,3,1,0:T(8,128)(2,1)S(1)} %bitcast.79) | data formatting | bytes 2958336 | tf_op jit(solution)/shard_map/all_to_all | solution.py:65
  1061.7 13.2 %reshape.95 = bf16[2,3,123264]{2,0,1:T(2,128)(2,1)} reshape(bf16[2,3,2568,2,24]{4,3,2,0,1:T(2,128)(2,1)} %copy.113) | data formatting | bytes 2958336 | tf_op jit(solution)/shard_map/reshape | solution.py:68
  1074.9 1.3 copy.110
  1076.1 1.3 all_to_all.61
  1078.2 13.1 %gather_fusion = bf16[400,128,144]{1,2,0:T(8,128)(2,1)} fusion(bf16[21,128,144]{1,2,0:T(8,128)(2,1)S(1)} %concatenate.13, s32[1024]{0:T(1024)S(1)} %pad_clamp_fusion), kind=kCustom, calls=%fused_computation | custom fusion | bytes 29492800 | tf_op jit(solution)/shard_map/gather | solution.py:86
  1091.3 15.2 %convolution_convert_fusion = bf16[400,6,24,64]{3,2,1,0:T(8,128)(2,1)} fusion(bf16[400,128,6,24]{1,3,2,0:T(8,128)(2,1)} %bitcast.71, bf16[400,64,128]{2,1,0:T(8,128)(2,1)} %param.9), kind=kOutput, calls=%fused_computation.27 | convolution fusion | flops 947404800 | bytes 28672000 | tf_op jit(solution)/shard_map/knj,kjcl->kcln/dot_general | solution.py:87
  1106.5 18.3 %copy.112 = bf16[400,6,24,64]{0,3,2,1:T(8,128)(2,1)} copy(bf16[400,6,24,64]{3,2,1,0:T(8,128)(2,1)} %convolution_convert_fusion) | data formatting | bytes 14745600 | tf_op jit(solution)/shard_map/convert_element_type | solution.py:88
  1124.8 11.3 copy.114
  (30 shorter events, 4.5 us)
Async XLA Ops:
  29.9 17.6 %copy-start.1 = (s32[400]{0:T(512)S(1)}, s32[400]{0:T(512)}, u32[]{:S(2)}) copy-start(s32[400]{0:T(512)} %param.10) | copy-start | bytes 4804
  47.5 48.4 %copy-start = (s32[1280]{0:T(1024)S(1)}, s32[1280]{0:T(1024)}, u32[]{:S(2)}) copy-start(s32[1280]{0:T(1024)} %param.11) | copy-start | bytes 15364
  84.8 22.7 %copy-start.2 = (s32[2]{0:T(128)S(1)}, s32[2]{0:T(128)}, u32[]{:S(2)}) copy-start(s32[2]{0:T(128)} %param.12) | copy-start | bytes 28
  84.8 760.7 %all-to-all-start = ((bf16[64,2,2880]{2,1,0:T(2,128)(2,1)}), bf16[64,2,2880]{2,1,0:T(2,128)(2,1)S(1)}, u32[]{:S(2)}, u32[]{:S(2)}) async-start(bf16[64,2,2880]{2,1,0:T(2,128)(2,1)} %reshape.111), calls=%async_computation | async-start | bytes 1507328 | tf_op jit(solution)/shard_map/all_to_all | solution.py:57
  1013.7 19.8 %copy-start.3 = (f32[2]{0:T(128)S(1)}, f32[2]{0:T(128)}, u32[]{:S(2)}) copy-start(f32[2]{0:T(128)} %param.13) | copy-start | bytes 28
  1036.4 38.5 %all-to-all-start.3 = ((bf16[1280,2,144]{2,1,0:T(2,128)(2,1)}), bf16[1280,2,144]{2,1,0:T(2,128)(2,1)S(1)}, u32[]{:S(2)}, u32[]{:S(2)}) async-start(bf16[1280,2,144]{2,1,0:T(2,128)(2,1)} %copy.109), calls=%async_computation.3 | async-start | bytes 2621440 | tf_op jit(solution)/shard_map/all_to_all | solution.py:82
where the time goes:
time: 1150 us; the launch traced here: 1140 us
  other arithmetic  750 us (65%)
  local copies, waits for them, and re-layouts  219 us (19%)
  matrix products  99.5 us (9%)
  blocking collectives  44.1 us (4%)
  starting transfers between devices  22.1 us (2%)
    another operation x2, other arithmetic  738 us
    unnamed x14, local copies, waits for them, and re-layouts  65 us
    all_to_all x2, local copies, waits for them, and re-layouts, local(): lax.all_to_all(grid_local, 'lev', split_axis=2, concat_axis=3, tiled=True)  31.3 us
    dot_general x1, matrix products, local(): jnp.einsum('ks,kjcl->sjcl', onehot, products, precision=lax.Precision.HIG...  24.5 us
  transfers between devices with their start and end apart: 2, of which 0 were waited for; matrix products, arithmetic and copies ran while one was open for 68% of the time, Pallas kernels for 0%

commit v1 on v0

v1 whole, which is shorter than its diff:
```python
import functools
import math

import jax
import jax.numpy as jnp
from jax import lax
from jax.experimental import pallas as pl
from jax.experimental.pallas import tpu as pltpu
from jax.sharding import PartitionSpec as P

MMAX = 1280
NLON = 5136
NBLK = 64
WAVES = 64
SLOTS = 20
HALF = NLON // 2
PAYLOAD = 2880
ROWS = 24
QUARTER = 1296
TILE = 432
FINE = 48
COARSE = QUARTER // FINE
OUTR = 336

f32 = jnp.float32
bf16 = jnp.bfloat16


def params(mib):
    return pltpu.CompilerParams(vmem_limit_bytes=mib * 1024 * 1024)


def block_diagonal(block):
    zero = jnp.zeros_like(block)
    return jnp.concatenate(
        [jnp.concatenate([block, zero], axis=1), jnp.concatenate([zero, block], axis=1)], axis=0
    )


def synthesis_kernel(slot_ref, spec_ref, leg_ref, out_ref, acc, stage, packed, rows, *, group):
    step = pl.program_id(0)

    @pl.when(step == 0)
    def _():
        acc[...] = jnp.zeros_like(acc)
        packed[...] = jnp.zeros_like(packed)

    blocks = spec_ref.shape[1]

    def body(g, carry):
        base = pl.multiple_of(g * group, group)
        for c in range(6):
            x = spec_ref[c, pl.ds(base, group), :].astype(f32)
            for t in range(12):
                stage[pl.ds(c * 12 + t, group, stride=72), :] = x[:, t * 128 : (t + 1) * 128]
        for kk in range(group):
            x = stage[kk * 72 : (kk + 1) * 72, :].astype(bf16)
            w = block_diagonal(leg_ref[base + kk])
            prod = jnp.dot(x, w, preferred_element_type=f32)
            slot = slot_ref[step * blocks + base + kk]
            acc[slot, 0:72, :] += prod[:, :128]
            acc[slot, 72:144, :] += prod[:, 128:]
        return carry

    lax.fori_loop(0, blocks // group, body, 0)

    @pl.when(step == pl.num_programs(0) - 1)
    def _():
        for q in range(SLOTS):
            for r in range(2):
                for l2 in range(2):
                    packed[pl.ds((q * 2 + r) * 72 + l2, 36, stride=2), :] = acc[
                        q, l2 * 72 + r * 36 : l2 * 72 + r * 36 + 36, :
                    ]
        for i in range(ROWS):
            rows[pl.ds(i, 128, stride=ROWS), :] = packed[i * 128 : (i + 1) * 128, :].T
        out_ref[...] = rows[...].astype(bf16)


def synthesis(block_slot, spec, legendre):
    count = spec.shape[1]
    blocks = 80
    group = 16
    return pl.pallas_call(
        functools.partial(synthesis_kernel, group=group),
        grid_spec=pltpu.PrefetchScalarGridSpec(
            num_scalar_prefetch=1,
            grid=(count // blocks,),
            in_specs=[
                pl.BlockSpec((6, blocks, 24 * NBLK), lambda i, s: (0, i, 0)),
                pl.BlockSpec((blocks, NBLK, 128), lambda i, s: (i, 0, 0)),
            ],
            out_specs=pl.BlockSpec((128 * ROWS, 128), lambda i, s: (0, 0)),
            scratch_shapes=[
                pltpu.VMEM((SLOTS + 1, 144, 128), f32),
                pltpu.VMEM((group * 72, 128), f32),
                pltpu.VMEM((ROWS * 128, 128), f32),
                pltpu.VMEM((ROWS * 128, 128), f32),
            ],
        ),
        out_shape=jax.ShapeDtypeStruct((128 * ROWS, 128), bf16),
        compiler_params=params(40),
        name="synthesis",
    )(block_slot, spec, legendre)


def analysis_kernel(slot_ref, in_ref, leg_ref, out_ref, coef, stage, packed, rows, *, group):
    step = pl.program_id(0)

    @pl.when(step == 0)
    def _():
        rows[...] = in_ref[...].astype(f32)
        for i in range(ROWS - 1):
            packed[i * 128 : (i + 1) * 128, :] = rows[pl.ds(i, 128, stride=ROWS), :].T
        for q in range(SLOTS):
            for l2 in range(2):
                for r in range(2):
                    stage[r * 36 : r * 36 + 36, :] = packed[
                        pl.ds((q * 2 + r) * 72 + l2, 36, stride=2), :
                    ]
                coef[q, 0:72, l2 * 128 : (l2 + 1) * 128] = stage[0:72, :].astype(bf16)
        coef[SLOTS] = jnp.zeros(coef.shape[1:], bf16)

    blocks = out_ref.shape[1]

    def body(g, carry):
        base = pl.multiple_of(g * group, group)
        for kk in range(group):
            slot = slot_ref[step * blocks + base + kk]
            w = block_diagonal(leg_ref[base + kk])
            stage[kk * 72 : (kk + 1) * 72, :] = lax.dot_general(
                coef[slot], w, (((1,), (1,)), ((), ())), preferred_element_type=f32
            )[:72]
        for c in range(6):
            for t in range(12):
                out_ref[c, pl.ds(base, group), t * 128 : (t + 1) * 128] = stage[
                    pl.ds(c * 12 + t, group, stride=72), :
                ].astype(bf16)
        return carry

    lax.fori_loop(0, blocks // group, body, 0)


def analysis(block_slot, payload, legendre):
    count = legendre.shape[0]
    blocks = 80
    group = 16
    return pl.pallas_call(
        functools.partial(analysis_kernel, group=group),
        grid_spec=pltpu.PrefetchScalarGridSpec(
            num_scalar_prefetch=1,
            grid=(count // blocks,),
            in_specs=[
                pl.BlockSpec((128 * ROWS, 128), lambda i, s: (0, 0)),
                pl.BlockSpec((blocks, NBLK, 128), lambda i, s: (i, 0, 0)),
            ],
            out_specs=pl.BlockSpec((6, blocks, 24 * NBLK), lambda i, s: (0, i, 0)),
            scratch_shapes=[
                pltpu.VMEM((SLOTS + 1, 80, 256), bf16),
                pltpu.VMEM((group * 72, 128), f32),
                pltpu.VMEM((ROWS * 128, 128), f32),
                pltpu.VMEM((ROWS * 128, 128), f32),
            ],
        ),
        out_shape=jax.ShapeDtypeStruct((6, count, 24 * NBLK), bf16),
        compiler_params=params(40),
        name="analysis",
    )(block_slot, payload, legendre)


def cosine_sine(phase, points, inverse):
    turns = jnp.floor(phase * inverse + 0.5)
    rest = phase - turns * points
    quarter = jnp.floor(4.0 * rest * inverse + 0.5)
    z = (4.0 * rest - quarter * points) * inverse * (0.5 * math.pi)
    z2 = z * z
    s = z * (1.0 + z2 * (-1 / 6 + z2 * (1 / 120 + z2 * (-1 / 5040 + z2 * (1 / 362880)))))
    c = 1.0 + z2 * (-0.5 + z2 * (1 / 24 + z2 * (-1 / 720 + z2 * (1 / 40320))))
    odd = jnp.abs(quarter) == 1.0
    flip = jnp.abs(quarter) == 2.0
    first = jnp.where(odd, s, c)
    second = jnp.where(odd, c, s)
    cos_sign = jnp.where(flip | (quarter == 1.0), -1.0, 1.0)
    sin_sign = jnp.where(flip | (quarter == -1.0), -1.0, 1.0)
    return first * cos_sign, second * sin_sign


def table_kernel(points_ref, m_ref, out_ref, fine_c, fine_s, coarse_c, coarse_s):
    step = pl.program_id(0)
    points = jnp.full((1, MMAX), points_ref[0], jnp.int32).astype(f32)
    inverse = 1.0 / points

    @pl.when(step == 0)
    def _():
        m = m_ref[...].astype(f32)
        live = jnp.where(2.0 * m < points, 1.0, 0.0)
        for base in range(0, FINE, 8):
            index = (base + lax.broadcasted_iota(jnp.int32, (8, MMAX), 0)).astype(f32)
            c, s = cosine_sine(index * m, points, inverse)
            fine_c[base : base + 8, :] = c
            fine_s[base : base + 8, :] = s
        for base in range(0, coarse_c.shape[0], 8):
            index = (FINE * (base + lax.broadcasted_iota(jnp.int32, (8, MMAX), 0))).astype(f32)
            c, s = cosine_sine(index * m, points, inverse)
            coarse_c[base : base + 8, :] = c * live
            coarse_s[base : base + 8, :] = s * live

    each = out_ref.shape[0] // FINE
    for b in range(each):
        row = step * each + b
        for lane in range(0, MMAX, 256):
            at = slice(lane, lane + 256)
            cb = coarse_c[pl.ds(row, 1), at]
            sb = coarse_s[pl.ds(row, 1), at]
            cf = fine_c[:, at]
            sf = fine_s[:, at]
            out_ref[b * FINE : (b + 1) * FINE, at] = (cb * cf - sb * sf).astype(bf16)
            out_ref[b * FINE : (b + 1) * FINE, MMAX + lane : MMAX + lane + 256] = (
                -(sb * cf + cb * sf)
            ).astype(bf16)


def tables(points, m_row):
    each = 3 * FINE
    return pl.pallas_call(
        table_kernel,
        grid_spec=pltpu.PrefetchScalarGridSpec(
            num_scalar_prefetch=1,
            grid=(QUARTER // each,),
            in_specs=[pl.BlockSpec((1, MMAX), lambda i, s: (0, 0))],
            out_specs=pl.BlockSpec((each, 2 * MMAX), lambda i, s: (i, 0)),
            scratch_shapes=[
                pltpu.VMEM((FINE, MMAX), f32),
                pltpu.VMEM((FINE, MMAX), f32),
                pltpu.VMEM((32, MMAX), f32),
                pltpu.VMEM((32, MMAX), f32),
            ],
        ),
        out_shape=jax.ShapeDtypeStruct((QUARTER, 2 * MMAX), bf16),
        compiler_params=params(24),
        name="tables",
    )(points, m_row)


def rotation(m):
    k = m & 3
    a = jnp.where(k == 0, 1.0, jnp.where(k == 2, -1.0, 0.0))
    b = jnp.where(k == 1, 1.0, jnp.where(k == 3, -1.0, 0.0))
    sign = jnp.where((k & 1) == 0, 1.0, -1.0)
    return a.astype(f32), b.astype(f32), sign.astype(f32)


def cycle_kernel(
    scalar_ref, weight_ref, in_ref, m_ref, table_ref, ret_ref, keep_ref, send_ref,
    rows, packed, coef, flux, grid,
):
    points = scalar_ref[0]
    lev = scalar_ref[1]
    quarter = points >> 2
    low = lax.broadcasted_iota(jnp.int32, (72, 128), 1) < 64

    rows[...] = in_ref[...].astype(f32)
    for i in range(ROWS - 1):
        block = jnp.concatenate(
            [
                rows[pl.ds(i, WAVES, stride=2 * ROWS), :],
                rows[pl.ds(ROWS + i, WAVES, stride=2 * ROWS), :],
            ],
            axis=0,
        )
        packed[i * 128 : (i + 1) * 128, :] = block.T

    for i in range(SLOTS // 2):
        lanes = slice(i * 128, (i + 1) * 128)
        m = m_ref[:, lanes]
        factor = jnp.where(m == 0, 1.0, 2.0).astype(f32)
        a, b, sign = rotation(m)
        parts = []
        for r in range(2):
            even = packed[(4 * i + r) * 72 : (4 * i + r + 1) * 72, :]
            odd = packed[(4 * i + 2 + r) * 72 : (4 * i + 3 + r) * 72, :]
            first = jnp.where(low, even, pltpu.roll(odd, 64, 1)) * factor
            second = jnp.where(low, pltpu.roll(even, 64, 1), odd) * factor
            parts.append((first, second))
        (re0, re1), (im0, im1) = parts
        for f in range(3):
            at = slice(f * 24, (f + 1) * 24)
            re = jnp.concatenate([re0[at], re1[at]], axis=0)
            im = jnp.concatenate([im0[at], im1[at]], axis=0)
            turned = [
                (re, im),
                (a * re - b * im, a * im + b * re),
                (sign * re, sign * im),
                (a * re + b * im, a * im - b * re),
            ]
            for r4 in range(4):
                out = slice(f * 192 + r4 * 48, f * 192 + (r4 + 1) * 48)
                coef[out, i * 128 : (i + 1) * 128] = turned[r4][0].astype(bf16)
                coef[out, MMAX + i * 128 : MMAX + (i + 1) * 128] = turned[r4][1].astype(bf16)

    tiles = QUARTER // TILE

    def inverse(step, carry):
        start = pl.multiple_of((tiles - 1 - step) * TILE, 16)
        values = lax.dot_general(
            table_ref[pl.ds(start, TILE), :], coef[...], (((1,), (1,)), ((), ())),
            preferred_element_type=f32,
        )
        index = start + lax.broadcasted_iota(jnp.int32, (TILE, 192), 0)
        fields = [
            jnp.where(index < quarter, values[:, f * 192 : (f + 1) * 192], 0.0)
            .astype(bf16)
            .astype(f32)
            for f in range(3)
        ]
        for f in range(3):
            for r4 in range(4):
                grid[f, pl.ds(r4 * quarter + start, TILE), 0:48] = fields[f][
                    :, r4 * 48 : (r4 + 1) * 48
                ]
        products = [fields[0] * fields[2], fields[1] * fields[2], 0.5 * fields[2] * fields[2]]
        for f in range(3):
            flux[step, f * 192 : (f + 1) * 192, :] = products[f].T.astype(bf16)
        return carry

    lax.fori_loop(0, tiles, inverse, 0)

    chunk = 48
    for which, ref in ((0, keep_ref), (1, send_ref)):
        half = lev if which == 0 else 1 - lev

        def place(j, carry, half=half, ref=ref):
            for f in range(3):
                pieces = []
                for s in range(8):
                    first = half * HALF + j * (8 * chunk) + s
                    piece = grid[f, pl.ds(first, chunk, stride=8), :][:, 0:48]
                    place_of = first + 8 * lax.broadcasted_iota(jnp.int32, (chunk, 48), 0)
                    pieces.append(jnp.where(place_of < points, piece, 0.0))
                ref[f, pl.ds(pl.multiple_of(j * chunk, 16), chunk), :] = jnp.concatenate(
                    pieces, axis=1
                ).astype(bf16)
            return carry

        lax.fori_loop(0, OUTR // chunk, place, 0)

    weight = weight_ref[0]

    def forward(n, carry):
        at = pl.multiple_of(n * 256, 256)
        cos_sum = jnp.zeros((576, 256), f32)
        sin_sum = jnp.zeros((576, 256), f32)
        for step in range(tiles):
            start = (tiles - 1 - step) * TILE
            cos_sum += jnp.dot(
                flux[step], table_ref[start : start + TILE, pl.ds(at, 256)],
                preferred_element_type=f32,
            )
            sin_sum += jnp.dot(
                flux[step], table_ref[start : start + TILE, pl.ds(at + MMAX, 256)],
                preferred_element_type=f32,
            )
        for i2 in range(2):
            lanes = slice(i2 * 128, (i2 + 1) * 128)
            a, b, sign = rotation(m_ref[:, pl.ds(at + i2 * 128, 128)])
            result = [[], []]
            for f in range(3):
                c = [cos_sum[f * 192 + r4 * 48 : f * 192 + (r4 + 1) * 48, lanes] for r4 in range(4)]
                s = [sin_sum[f * 192 + r4 * 48 : f * 192 + (r4 + 1) * 48, lanes] for r4 in range(4)]
                result[0].append(
                    (c[0] + sign * c[2] + a * (c[1] + c[3]) + b * (s[1] - s[3])) * weight
                )
                result[1].append(
                    (s[0] + sign * s[2] + a * (s[1] + s[3]) - b * (c[1] - c[3])) * weight
                )
            for r in range(2):
                first = jnp.concatenate([x[:24] for x in result[r]], axis=0)
                second = jnp.concatenate([x[24:] for x in result[r]], axis=0)
                row = pl.multiple_of((n * 8 + 4 * i2 + r) * 72, 8)
                packed[pl.ds(row, 72), :] = jnp.where(low, first, pltpu.roll(second, 64, 1))
                packed[pl.ds(row + 144, 72), :] = jnp.where(low, pltpu.roll(first, 64, 1), second)
        return carry

    lax.fori_loop(0, MMAX // 256, forward, 0)

    for i in range(ROWS):
        if i == ROWS - 1:
            block = jnp.zeros((128, 128), f32)
        else:
            block = packed[i * 128 : (i + 1) * 128, :].T
        rows[pl.ds(i, WAVES, stride=2 * ROWS), :] = block[:64]
        rows[pl.ds(ROWS + i, WAVES, stride=2 * ROWS), :] = block[64:]
    ret_ref[...] = rows[...].astype(bf16)


def cycle(scalars, weight, payload, m_row, table):
    return pl.pallas_call(
        cycle_kernel,
        in_specs=[
            pl.BlockSpec(memory_space=pltpu.SMEM),
            pl.BlockSpec(memory_space=pltpu.SMEM),
            pl.BlockSpec(memory_space=pltpu.VMEM),
            pl.BlockSpec(memory_space=pltpu.VMEM),
            pl.BlockSpec(memory_space=pltpu.VMEM),
        ],
        out_specs=[pl.BlockSpec(memory_space=pltpu.VMEM)] * 3,
        out_shape=[
            jax.ShapeDtypeStruct((128 * ROWS, 128), bf16),
            jax.ShapeDtypeStruct((3, OUTR, 384), bf16),
            jax.ShapeDtypeStruct((3, OUTR, 384), bf16),
        ],
        scratch_shapes=[
            pltpu.VMEM((128 * ROWS, 128), f32),
            pltpu.VMEM((128 * ROWS, 128), f32),
            pltpu.VMEM((576, 2 * MMAX), bf16),
            pltpu.VMEM((QUARTER // TILE, 576, TILE), bf16),
            pltpu.VMEM((3, 5264, 128), f32),
        ],
        compiler_params=params(56),
        name="cycle",
    )(scalars, weight, payload, m_row, table)


def local(spectra, legendre, block_slot, wavenumber, cycle_points, quad_weight):
    lev = lax.axis_index("lev")
    spec = jnp.transpose(spectra, (1, 0, 2))
    sent = synthesis(block_slot, spec, legendre).reshape(128, ROWS, 128)
    received = lax.all_to_all(sent, ("wave", "lev"), split_axis=0, concat_axis=0, tiled=True)
    points = lax.dynamic_slice(cycle_points, (lev,), (1,))
    weight = lax.dynamic_slice(quad_weight, (lev,), (1,))
    m_row = wavenumber.reshape(WAVES, SLOTS).T.reshape(1, MMAX)
    table = tables(points, m_row)
    scalars = jnp.concatenate([points, lev[None].astype(jnp.int32)])
    ret, keep, send = cycle(scalars, weight, received.reshape(128 * ROWS, 128), m_row, table)
    other = lax.ppermute(send, "lev", [(0, 1), (1, 0)])
    returned = lax.all_to_all(
        ret.reshape(128, ROWS, 128), ("wave", "lev"), split_axis=0, concat_axis=0, tiled=True
    )
    tendency = analysis(block_slot, returned.reshape(128 * ROWS, 128), legendre)
    own_first = lev == 0
    both = jnp.stack(
        [jnp.where(own_first, keep, other), jnp.where(own_first, other, keep)], axis=0
    )
    grid_fields = both[:, :, : HALF // 8, :].reshape(2, 3, HALF * 48)
    return (jnp.transpose(tendency, (1, 0, 2)), grid_fields)


def solution(mesh):
    placed = (P("wave", None, "lev"), P("wave", None, None), P("wave"), P(), P("wave"), P("wave"))
    return jax.shard_map(
        local,
        mesh=mesh,
        in_specs=placed,
        out_specs=(P("wave", None, "lev"), P("wave", None, "lev")),
        check_vma=False,
    )
```

time: 1150 us -> 119 us (0.10); the launches traced: 1140 us -> 118 us
  other arithmetic: 750 us -> 2.75 us
  local copies, waits for them, and re-layouts: 219 us -> 14.6 us
  matrix products: 99.5 us -> 0 us
  Pallas kernels: 0 us -> 55.4 us
  blocking collectives: 44.1 us -> 0 us
  waiting for transfers between devices: 0.01 us -> 27.2 us
    another operation x3 -> x2, other arithmetic: 738 us -> 1.45 us  [local(): jnp.stack([jnp.where(own_first, keep, other), jnp.where(own_first, other,...]
    dot_general x4 -> x0, matrix products: 79.8 us -> none  [the longest x1 24.5 us: local(): jnp.einsum('ks,kjcl->sjcl', onehot, products, precision=lax.Precision.HIG...]
    all_to_all x10 -> x0, local copies, waits for them, and re-layouts: 60.9 us -> none  [the longest x2 31.3 us: local(): lax.all_to_all(grid_local, 'lev', split_axis=2, concat_axis=3, tiled=True)]
    pallas_call x0 -> x4, Pallas kernels: none -> 55.4 us  [the longest x1 23.4 us: cycle(): pl.pallas_call(cycle_kernel, in_specs=[pl.BlockSpec(memory_space=pltpu.SM...]
    unnamed x14 -> x20, local copies, waits for them, and re-layouts: 65 us -> 10.1 us
    all_to_all x2 -> x0, blocking collectives: 44.1 us -> none  [the longest x1 22.8 us: local(): lax.all_to_all(grid_local, 'lev', split_axis=2, concat_axis=3, tiled=True)]
    convert_element_type x5 -> x0, local copies, waits for them, and re-layouts: 38.8 us -> none  [the longest x1 18.3 us: local(): tendency.reshape(block_count, 6, lev_count * degree_count)]
    reshape x4 -> x3, local copies, waits for them, and re-layouts: 40 us -> 3.04 us  [the longest x1 2.86 us: local(): grid_fields = both[:, :, :HALF // 8, :].reshape(2, 3, HALF * 48)]
  transfers between devices with their start and end apart: 2 -> 3, of which waited for: 0 -> 3; matrix products, arithmetic and copies ran while one was open for 68% -> 6% of each run, Pallas kernels for 0% -> 3%
where the time goes in v1:
time: 119 us; the launch traced here: 118 us
  Pallas kernels  55.4 us (47%)
  waiting for transfers between devices  27.2 us (23%)
  starting transfers between devices  17.4 us (15%)
  local copies, waits for them, and re-layouts  14.6 us (12%)
  other arithmetic  2.75 us (2%)
    pallas_call x1, Pallas kernels, cycle(): pl.pallas_call(cycle_kernel, in_specs=[pl.BlockSpec(memory_space=pltpu.SM...  23.4 us
    pallas_call x1, Pallas kernels, analysis(): pl.pallas_call(functools.partial(analysis_kernel, group=group), grid_spec...  16.1 us
    ppermute x1, waiting for transfers between devices, local(): other = lax.ppermute(send, 'lev', [(0, 1), (1, 0)])  14.2 us
    pallas_call x1, Pallas kernels, synthesis(): pl.pallas_call(functools.partial(synthesis_kernel, group=group), grid_spe...  12.7 us
    all_to_all x1, starting transfers between devices, local(): lax.all_to_all(sent, ('wave', 'lev'), split_axis=0, concat_axis=0, tiled=...  11.5 us
    unnamed x20, local copies, waits for them, and re-layouts  10.1 us
    all_to_all x1, waiting for transfers between devices, local(): lax.all_to_all(sent, ('wave', 'lev'), split_axis=0, concat_axis=0, tiled=...  7.76 us
    all_to_all x1, waiting for transfers between devices, local(): lax.all_to_all(ret.reshape(128, ROWS, 128), ('wave', 'lev'), split_axis=0...  5.25 us
  transfers between devices with their start and end apart: 3, of which 3 were waited for; matrix products, arithmetic and copies ran while one was open for 6% of the time, Pallas kernels for 3%

profile of v1, /device:TPU:1, one launch (start us, length us, event | category | flops | bytes accessed | tf_op | source)
XLA Modules:
  0.0 118.2 jit_solution(8640673431924232415)
XLA Ops:
  0.6 0.0 copy-start.1
  0.6 2.9 %copy-done.1 = bf16[400,64,128]{2,1,0:T(8,128)(2,1)S(1)} copy-done((bf16[400,64,128]{2,1,0:T(8,128)(2,1)S(1)}, bf16[400,64,128]{2,1,0:T(8,128)(2,1)}, u32[]{:S(2)}) %copy-start.1) | copy-done | bytes 6553624
  3.5 0.7 copy-done.4
  4.2 12.7 %synthesis.1 = bf16[3072,128]{1,0:T(8,128)(2,1)} custom-call(s32[400]{0:T(512)S(1)} %copy-done.4, bf16[6,400,1536]{2,1,0:T(8,128)(2,1)} %bitcast.15, bf16[400,64,128]{2,1,0:T(8,128)(2,1)S(1)} %copy-done.1), custom_call_target="tpu_custom_call" | custom-call | tf_op jit(solution)/shard_map/synthesis/pallas_call | solution.py:84
  16.9 11.5 %all-to-all-start = ((bf16[128,24,128]{2,1,0:T(8,128)(2,1)}), bf16[128,24,128]{2,1,0:T(8,128)(2,1)S(1)}, u32[]{:S(2)}, u32[]{:S(2)}) async-start(bf16[128,24,128]{2,1,0:T(8,128)(2,1)} %bitcast.2), calls=%async_computation | async-start | bytes 1572864 | tf_op jit(solution)/shard_map/all_to_all | solution.py:428
  28.4 0.0 copy-done.8
  28.4 0.7 dynamic_slice.7.weight_ref
  29.0 0.0 copy-done.9
  29.0 0.6 dynamic_slice.6.points_ref
  29.6 0.0 copy-done.7
  29.6 0.1 reshape.27
  29.7 0.1 copy.9
  29.8 0.1 reshape.28.m_ref
  29.9 3.2 %tables.1.table_ref = bf16[1296,2560]{1,0:T(8,128)(2,1)S(1)} custom-call(s32[1]{0:T(128)} %dynamic_slice.6.points_ref, s32[1,1280]{1,0:T(1,128)S(1)} %reshape.28.m_ref), custom_call_target="tpu_custom_call" | custom-call | tf_op jit(solution)/shard_map/tables/pallas_call | solution.py:225
  33.1 0.0 copy-start
  33.1 2.8 %copy-done = bf16[1296,2560]{1,0:T(8,128)(2,1)} copy-done((bf16[1296,2560]{1,0:T(8,128)(2,1)}, bf16[1296,2560]{1,0:T(8,128)(2,1)S(1)}, u32[]{:S(2)}) %copy-start) | copy-done | bytes 6635544
  35.9 1.3 %pad_add_fusion.scalar_ref = s32[2]{0:T(128)} fusion(s32[1]{0:T(128)} %bitcast, s32[1]{0:T(128)} %dynamic_slice.6.points_ref), kind=kLoop, calls=%fused_computation.3 | loop fusion | flops 2 | bytes 16 | tf_op jit(solution)/shard_map/concatenate | solution.py:433
  37.2 7.8 %all-to-all-done = bf16[128,24,128]{2,1,0:T(8,128)(2,1)S(1)} async-done(((bf16[128,24,128]{2,1,0:T(8,128)(2,1)}), bf16[128,24,128]{2,1,0:T(8,128)(2,1)S(1)}, u32[]{:S(2)}, u32[]{:S(2)}) %all-to-all-start) | async-done | bytes 786464 | tf_op jit(solution)/shard_map/all_to_all | solution.py:428
  45.0 0.9 copy-done.6
  45.9 23.4 %cycle.1 = (bf16[3072,128]{1,0:T(8,128)(2,1)}, bf16[3,336,384]{2,1,0:T(8,128)(2,1)}, bf16[3,336,384]{2,1,0:T(8,128)(2,1)}) custom-call(s32[2]{0:T(128)} %pad_add_fusion.scalar_ref, f32[1]{0:T(128)} %dynamic_slice.7.weight_ref, bf16[3072,128]{1,0:T(8,128)(2,1)} %bitcast.17, s32[1,1280]{1,0:T(1,128)} %copy-done.3, bf16[1296,2560]{1,0:T(8,128)(2,1)} %copy-done), custom_call_target="tpu_custom_call" | custom-call | tf_op jit(solution)/shard_map/cycle/pallas_call | solution.py:397
  69.3 0.8 collective-permute-start
  70.1 5.2 %all-to-all-start.1 = ((bf16[128,24,128]{2,1,0:T(8,128)(2,1)}), bf16[128,24,128]{2,1,0:T(8,128)(2,1)S(1)}, u32[]{:S(2)}, u32[]{:S(2)}) async-start(bf16[128,24,128]{2,1,0:T(8,128)(2,1)} %bitcast.18), calls=%async_computation.1 | async-start | bytes 1572864 | tf_op jit(solution)/shard_map/all_to_all | solution.py:436
  75.2 14.2 %collective-permute-done = bf16[3,336,384]{2,1,0:T(8,128)(2,1)S(1)} collective-permute-done((bf16[3,336,384]{2,1,0:T(8,128)(2,1)}, bf16[3,336,384]{2,1,0:T(8,128)(2,1)S(1)}, u32[]{:S(2)}, u32[]{:S(2)}) %collective-permute-start) | collective-permute-done | bytes 774176 | tf_op jit(solution)/shard_map/ppermute | solution.py:435
  89.5 1.3 %select_bitcast_fusion.1 = (bf16[1,3,336,384]{3,2,1,0:T(8,128)(2,1)S(1)}, bf16[1,3,336,384]{3,2,1,0:T(8,128)(2,1)S(1)}) fusion(bf16[3,336,384]{2,1,0:T(8,128)(2,1)} %get-tuple-element.6, bf16[3,336,384]{2,1,0:T(8,128)(2,1)S(1)} %collective-permute-done, pred[]{:T(512)S(6)} %eq.3), kind=kLoop, calls=%fused_computation.2 | loop fusion | flops 774144 | bytes 3096577 | tf_op jit(solution)/shard_map/stack | solution.py:441
  90.7 0.2 pad_maximum_fusion
  90.9 0.0 copy-start.5
  90.9 0.2 copy.10
  91.1 2.9 %reshape.31 = bf16[2,3,123264]{2,0,1:T(2,128)(2,1)} reshape(bf16[2,3,321,384]{3,2,0,1:T(8,128)(2,1)S(1)} %copy.10) | data formatting | bytes 2958336 | tf_op jit(solution)/shard_map/reshape | solution.py:444
  93.9 5.2 %all-to-all-done.1 = bf16[128,24,128]{2,1,0:T(8,128)(2,1)S(1)} async-done(((bf16[128,24,128]{2,1,0:T(8,128)(2,1)}), bf16[128,24,128]{2,1,0:T(8,128)(2,1)S(1)}, u32[]{:S(2)}, u32[]{:S(2)}) %all-to-all-start.1) | async-done | bytes 786464 | tf_op jit(solution)/shard_map/all_to_all | solution.py:436
  99.2 0.0 copy-done.5
  99.2 2.9 %copy-done.2 = bf16[400,64,128]{2,1,0:T(8,128)(2,1)S(1)} copy-done((bf16[400,64,128]{2,1,0:T(8,128)(2,1)S(1)}, bf16[400,64,128]{2,1,0:T(8,128)(2,1)}, u32[]{:S(2)}) %copy-start.2) | copy-done | bytes 6553624
  102.1 16.1 %analysis.1 = bf16[6,400,1536]{2,1,0:T(8,128)(2,1)} custom-call(s32[400]{0:T(512)S(1)} %copy-done.5, bf16[3072,128]{1,0:T(8,128)(2,1)S(1)} %bitcast.14, bf16[400,64,128]{2,1,0:T(8,128)(2,1)S(1)} %copy-done.2), custom_call_target="tpu_custom_call" | custom-call | tf_op jit(solution)/shard_map/analysis/pallas_call | solution.py:148
  (8 shorter events, 0.0 us)
Async XLA Ops:
  0.6 2.9 %copy-start.1 = (bf16[400,64,128]{2,1,0:T(8,128)(2,1)S(1)}, bf16[400,64,128]{2,1,0:T(8,128)(2,1)}, u32[]{:S(2)}) copy-start(bf16[400,64,128]{2,1,0:T(8,128)(2,1)} %leg_ref.3) | copy-start | bytes 19660804
  3.5 0.7 copy-start.4
  4.2 24.2 %copy-start.8 = (f32[2]{0:T(128)S(1)}, f32[2]{0:T(128)}, u32[]{:S(2)}) copy-start(f32[2]{0:T(128)} %param.11) | copy-start | bytes 28
  4.2 24.8 %copy-start.9 = (s32[2]{0:T(128)S(1)}, s32[2]{0:T(128)}, u32[]{:S(2)}) copy-start(s32[2]{0:T(128)} %param.10) | copy-start | bytes 28
  4.2 25.4 %copy-start.7 = (s32[1280]{0:T(1024)S(1)}, s32[1280]{0:T(1024)}, u32[]{:S(2)}) copy-start(s32[1280]{0:T(1024)} %param.9) | copy-start | bytes 15364
  16.9 28.2 %all-to-all-start = ((bf16[128,24,128]{2,1,0:T(8,128)(2,1)}), bf16[128,24,128]{2,1,0:T(8,128)(2,1)S(1)}, u32[]{:S(2)}, u32[]{:S(2)}) async-start(bf16[128,24,128]{2,1,0:T(8,128)(2,1)} %bitcast.2), calls=%async_computation | async-start | bytes 1572864 | tf_op jit(solution)/shard_map/all_to_all | solution.py:428
  29.9 3.2 %copy-start.3 = (s32[1,1280]{1,0:T(1,128)}, s32[1,1280]{1,0:T(1,128)S(1)}, u32[]{:S(2)}) copy-start(s32[1,1280]{1,0:T(1,128)S(1)} %reshape.28.m_ref) | copy-start | bytes 15364
  33.1 2.8 %copy-start = (bf16[1296,2560]{1,0:T(8,128)(2,1)}, bf16[1296,2560]{1,0:T(8,128)(2,1)S(1)}, u32[]{:S(2)}) copy-start(bf16[1296,2560]{1,0:T(8,128)(2,1)S(1)} %tables.1.table_ref) | copy-start | bytes 19906564
  45.0 0.9 copy-start.6
  69.3 20.2 %collective-permute-start = (bf16[3,336,384]{2,1,0:T(8,128)(2,1)}, bf16[3,336,384]{2,1,0:T(8,128)(2,1)S(1)}, u32[]{:S(2)}, u32[]{:S(2)}) collective-permute-start(bf16[3,336,384]{2,1,0:T(8,128)(2,1)} %get-tuple-element.7), channel_id=1, source_target_pairs={{0,1},{1,0},{2,3},{3,2},{4,5},{5,4},{6,7},{7,6},{8,9},{9,8},{10,11... | collective-permute-start | bytes 2322440 | tf_op jit(solution)/shard_map/ppermute | solution.py:435
  70.1 29.1 %all-to-all-start.1 = ((bf16[128,24,128]{2,1,0:T(8,128)(2,1)}), bf16[128,24,128]{2,1,0:T(8,128)(2,1)S(1)}, u32[]{:S(2)}, u32[]{:S(2)}) async-start(bf16[128,24,128]{2,1,0:T(8,128)(2,1)} %bitcast.18), calls=%async_computation.1 | async-start | bytes 1572864 | tf_op jit(solution)/shard_map/all_to_all | solution.py:436
  90.9 8.3 %copy-start.5 = (s32[400]{0:T(512)S(1)}, s32[400]{0:T(512)}, u32[]{:S(2)}) copy-start(s32[400]{0:T(512)} %slot_ref.3) | copy-start | bytes 4804
  99.2 2.9 %copy-start.2 = (bf16[400,64,128]{2,1,0:T(8,128)(2,1)S(1)}, bf16[400,64,128]{2,1,0:T(8,128)(2,1)}, u32[]{:S(2)}) copy-start(bf16[400,64,128]{2,1,0:T(8,128)(2,1)} %leg_ref.3) | copy-start | bytes 19660804

commit v2 on v1

--- a/solution.py
+++ b/solution.py
@@ -21,6 +21,9 @@
 FINE = 48
 COARSE = QUARTER // FINE
 OUTR = 336
+GROUP = 16
+RUNS = ((0, 32), (32, 96), (128, 96), (224, 96), (320, 80))
+STRIDE = 73
 
 f32 = jnp.float32
 bf16 = jnp.bfloat16
@@ -37,133 +40,156 @@
     )
 
 
-def synthesis_kernel(slot_ref, spec_ref, leg_ref, out_ref, acc, stage, packed, rows, *, group):
-    step = pl.program_id(0)
-
-    @pl.when(step == 0)
-    def _():
-        acc[...] = jnp.zeros_like(acc)
-        packed[...] = jnp.zeros_like(packed)
-
-    blocks = spec_ref.shape[1]
+def copy_in(spec_hbm, leg_hbm, spec, leg, sems):
+    copies = []
+    for n, (first, count) in enumerate(RUNS):
+        pair = [
+            pltpu.make_async_copy(
+                leg_hbm.at[pl.ds(first, count)], leg.at[pl.ds(first, count)], sems.at[0, n]
+            )
+        ]
+        if spec is not None:
+            pair.append(
+                pltpu.make_async_copy(
+                    spec_hbm.at[:, pl.ds(first, count)],
+                    spec.at[:, pl.ds(first, count)],
+                    sems.at[1, n],
+                )
+            )
+        for copy in pair:
+            copy.start()
+        copies.append(pair)
+    return copies
+
+
+def synthesis_kernel(
+    slot_ref, spec_hbm, leg_hbm, out_ref, spec, leg, sems, acc, stage, packed, rows
+):
+    copies = copy_in(spec_hbm, leg_hbm, spec, leg, sems)
+    acc[...] = jnp.zeros_like(acc)
+    packed[...] = jnp.zeros_like(packed)
 
     def body(g, carry):
-        base = pl.multiple_of(g * group, group)
+        base = pl.multiple_of(g * GROUP, GROUP)
         for c in range(6):
-            x = spec_ref[c, pl.ds(base, group), :].astype(f32)
+            x = spec[c, pl.ds(base, GROUP), :].astype(f32)
             for t in range(12):
-                stage[pl.ds(c * 12 + t, group, stride=72), :] = x[:, t * 128 : (t + 1) * 128]
-        for kk in range(group):
-            x = stage[kk * 72 : (kk + 1) * 72, :].astype(bf16)
-            w = block_diagonal(leg_ref[base + kk])
+                stage[pl.ds(c * 12 + t, GROUP, stride=STRIDE), :] = x[:, t * 128 : (t + 1) * 128]
+        for kk in range(GROUP):
+            x = stage[kk * STRIDE : kk * STRIDE + 72, :].astype(bf16)
+            w = block_diagonal(leg[base + kk])
             prod = jnp.dot(x, w, preferred_element_type=f32)
-            slot = slot_ref[step * blocks + base + kk]
+            slot = slot_ref[base + kk]
             acc[slot, 0:72, :] += prod[:, :128]
             acc[slot, 72:144, :] += prod[:, 128:]
         return carry
 
-    lax.fori_loop(0, blocks // group, body, 0)
-
-    @pl.when(step == pl.num_programs(0) - 1)
-    def _():
-        for q in range(SLOTS):
-            for r in range(2):
-                for l2 in range(2):
-                    packed[pl.ds((q * 2 + r) * 72 + l2, 36, stride=2), :] = acc[
-                        q, l2 * 72 + r * 36 : l2 * 72 + r * 36 + 36, :
-                    ]
-        for i in range(ROWS):
-            rows[pl.ds(i, 128, stride=ROWS), :] = packed[i * 128 : (i + 1) * 128, :].T
-        out_ref[...] = rows[...].astype(bf16)
+    for (first, count), pair in zip(RUNS, copies):
+        for copy in pair:
+            copy.wait()
+        lax.fori_loop(first // GROUP, (first + count) // GROUP, body, 0)
+
+    for q in range(SLOTS):
+        for r in range(2):
+            for l2 in range(2):
+                packed[pl.ds((q * 2 + r) * 72 + l2, 36, stride=2), :] = acc[
+                    q, l2 * 72 + r * 36 : l2 * 72 + r * 36 + 36, :
+                ]
+    for i in range(ROWS):
+        rows[pl.ds(i, 128, stride=ROWS), :] = packed[i * 128 : (i + 1) * 128, :].T
+    out_ref[...] = rows[...].astype(bf16)
 
 
 def synthesis(block_slot, spec, legendre):
-    count = spec.shape[1]
-    blocks = 80
-    group = 16
     return pl.pallas_call(
-        functools.partial(synthesis_kernel, group=group),
-        grid_spec=pltpu.PrefetchScalarGridSpec(
-            num_scalar_prefetch=1,
-            grid=(count // blocks,),
-            in_specs=[
-                pl.BlockSpec((6, blocks, 24 * NBLK), lambda i, s: (0, i, 0)),
-                pl.BlockSpec((blocks, NBLK, 128), lambda i, s: (i, 0, 0)),
-            ],
-            out_specs=pl.BlockSpec((128 * ROWS, 128), lambda i, s: (0, 0)),
-            scratch_shapes=[
-                pltpu.VMEM((SLOTS + 1, 144, 128), f32),
-                pltpu.VMEM((group * 72, 128), f32),
-                pltpu.VMEM((ROWS * 128, 128), f32),
-                pltpu.VMEM((ROWS * 128, 128), f32),
-            ],
-        ),
+        synthesis_kernel,
+        in_specs=[
+            pl.BlockSpec(memory_space=pltpu.SMEM),
+            pl.BlockSpec(memory_space=pl.ANY),
+            pl.BlockSpec(memory_space=pl.ANY),
+        ],
+        out_specs=pl.BlockSpec(memory_space=pltpu.VMEM),
+        scratch_shapes=[
+            pltpu.VMEM(spec.shape, bf16),
+            pltpu.VMEM(legendre.shape, bf16),
+            pltpu.SemaphoreType.DMA((2, len(RUNS))),
+            pltpu.VMEM((SLOTS + 1, 144, 128), f32),
+            pltpu.VMEM((GROUP * 80, 128), f32),
+            pltpu.VMEM((ROWS * 128, 128), f32),
+            pltpu.VMEM((ROWS * 128, 128), f32),
+        ],
         out_shape=jax.ShapeDtypeStruct((128 * ROWS, 128), bf16),
-        compiler_params=params(40),
+        compiler_params=params(60),
         name="synthesis",
     )(block_slot, spec, legendre)
 
 
-def analysis_kernel(slot_ref, in_ref, leg_ref, out_ref, coef, stage, packed, rows, *, group):
-    step = pl.program_id(0)
-
-    @pl.when(step == 0)
-    def _():
-        rows[...] = in_ref[...].astype(f32)
-        for i in range(ROWS - 1):
-            packed[i * 128 : (i + 1) * 128, :] = rows[pl.ds(i, 128, stride=ROWS), :].T
-        for q in range(SLOTS):
-            for l2 in range(2):
-                for r in range(2):
-                    stage[r * 36 : r * 36 + 36, :] = packed[
-                        pl.ds((q * 2 + r) * 72 + l2, 36, stride=2), :
-                    ]
-                coef[q, 0:72, l2 * 128 : (l2 + 1) * 128] = stage[0:72, :].astype(bf16)
-        coef[SLOTS] = jnp.zeros(coef.shape[1:], bf16)
-
-    blocks = out_ref.shape[1]
+def analysis_kernel(
+    slot_ref, in_ref, leg_hbm, out_hbm, leg, out, in_sems, out_sems, coef, stage, packed, rows
+):
+    copies = copy_in(None, leg_hbm, None, leg, in_sems)
+    rows[...] = in_ref[...].astype(f32)
+    for i in range(ROWS - 1):
+        packed[i * 128 : (i + 1) * 128, :] = rows[pl.ds(i, 128, stride=ROWS), :].T
+    for q in range(SLOTS):
+        for l2 in range(2):
+            for r in range(2):
+                stage[r * 36 : r * 36 + 36, :] = packed[
+                    pl.ds((q * 2 + r) * 72 + l2, 36, stride=2), :
+                ]
+            coef[q, 0:72, l2 * 128 : (l2 + 1) * 128] = stage[0:72, :].astype(bf16)
+    coef[SLOTS] = jnp.zeros(coef.shape[1:], bf16)
 
     def body(g, carry):
-        base = pl.multiple_of(g * group, group)
-        for kk in range(group):
-            slot = slot_ref[step * blocks + base + kk]
-            w = block_diagonal(leg_ref[base + kk])
-            stage[kk * 72 : (kk + 1) * 72, :] = lax.dot_general(
+        base = pl.multiple_of(g * GROUP, GROUP)
+        for kk in range(GROUP):
+            slot = slot_ref[base + kk]
+            w = block_diagonal(leg[base + kk])
+            stage[kk * STRIDE : kk * STRIDE + 72, :] = lax.dot_general(
                 coef[slot], w, (((1,), (1,)), ((), ())), preferred_element_type=f32
             )[:72]
         for c in range(6):
             for t in range(12):
-                out_ref[c, pl.ds(base, group), t * 128 : (t + 1) * 128] = stage[
-                    pl.ds(c * 12 + t, group, stride=72), :
+                out[c, pl.ds(base, GROUP), t * 128 : (t + 1) * 128] = stage[
+                    pl.ds(c * 12 + t, GROUP, stride=STRIDE), :
                 ].astype(bf16)
         return carry
 
-    lax.fori_loop(0, blocks // group, body, 0)
+    written = []
+    for n, (first, count) in enumerate(RUNS):
+        copies[n][0].wait()
+        lax.fori_loop(first // GROUP, (first + count) // GROUP, body, 0)
+        copy = pltpu.make_async_copy(
+            out.at[:, pl.ds(first, count)], out_hbm.at[:, pl.ds(first, count)], out_sems.at[n]
+        )
+        copy.start()
+        written.append(copy)
+    for copy in written:
+        copy.wait()
 
 
 def analysis(block_slot, payload, legendre):
-    count = legendre.shape[0]
-    blocks = 80
-    group = 16
+    shape = (6, legendre.shape[0], 24 * NBLK)
     return pl.pallas_call(
-        functools.partial(analysis_kernel, group=group),
-        grid_spec=pltpu.PrefetchScalarGridSpec(
-            num_scalar_prefetch=1,
-            grid=(count // blocks,),
-            in_specs=[
-                pl.BlockSpec((128 * ROWS, 128), lambda i, s: (0, 0)),
-                pl.BlockSpec((blocks, NBLK, 128), lambda i, s: (i, 0, 0)),
-            ],
-            out_specs=pl.BlockSpec((6, blocks, 24 * NBLK), lambda i, s: (0, i, 0)),
-            scratch_shapes=[
-                pltpu.VMEM((SLOTS + 1, 80, 256), bf16),
-                pltpu.VMEM((group * 72, 128), f32),
-                pltpu.VMEM((ROWS * 128, 128), f32),
-                pltpu.VMEM((ROWS * 128, 128), f32),
-            ],
-        ),
-        out_shape=jax.ShapeDtypeStruct((6, count, 24 * NBLK), bf16),
-        compiler_params=params(40),
+        analysis_kernel,
+        in_specs=[
+            pl.BlockSpec(memory_space=pltpu.SMEM),
+            pl.BlockSpec(memory_space=pltpu.VMEM),
+            pl.BlockSpec(memory_space=pl.ANY),
+        ],
+        out_specs=pl.BlockSpec(memory_space=pl.ANY),
+        scratch_shapes=[
+            pltpu.VMEM(legendre.shape, bf16),
+            pltpu.VMEM(shape, bf16),
+            pltpu.SemaphoreType.DMA((2, len(RUNS))),
+            pltpu.SemaphoreType.DMA((len(RUNS),)),
+            pltpu.VMEM((SLOTS + 1, 80, 256), bf16),
+            pltpu.VMEM((GROUP * 80, 128), f32),
+            pltpu.VMEM((ROWS * 128, 128), f32),
+            pltpu.VMEM((ROWS * 128, 128), f32),
+        ],
+        out_shape=jax.ShapeDtypeStruct(shape, bf16),
+        compiler_params=params(60),
         name="analysis",
     )(block_slot, payload, legendre)
 
@@ -250,9 +276,8 @@
     return a.astype(f32), b.astype(f32), sign.astype(f32)
 
 
-def cycle_kernel(
-    scalar_ref, weight_ref, in_ref, m_ref, table_ref, ret_ref, keep_ref, send_ref,
-    rows, packed, coef, flux, grid,
+def inverse_kernel(
+    scalar_ref, in_ref, m_ref, table_ref, flux, keep_ref, send_ref, rows, packed, coef, grid
 ):
     points = scalar_ref[0]
     lev = scalar_ref[1]
@@ -300,7 +325,7 @@
 
     tiles = QUARTER // TILE
 
-    def inverse(step, carry):
+    def tile(step, carry):
         start = pl.multiple_of((tiles - 1 - step) * TILE, 16)
         values = lax.dot_general(
             table_ref[pl.ds(start, TILE), :], coef[...], (((1,), (1,)), ((), ())),
@@ -323,7 +348,7 @@
             flux[step, f * 192 : (f + 1) * 192, :] = products[f].T.astype(bf16)
         return carry
 
-    lax.fori_loop(0, tiles, inverse, 0)
+    lax.fori_loop(0, tiles, tile, 0)
 
     chunk = 48
     for which, ref in ((0, keep_ref), (1, send_ref)):
@@ -344,9 +369,13 @@
 
         lax.fori_loop(0, OUTR // chunk, place, 0)
 
+
+def forward_kernel(weight_ref, m_ref, table_ref, flux, ret_ref, rows, packed):
+    low = lax.broadcasted_iota(jnp.int32, (72, 128), 1) < 64
+    tiles = QUARTER // TILE
     weight = weight_ref[0]
 
-    def forward(n, carry):
+    def columns(n, carry):
         at = pl.multiple_of(n * 256, 256)
         cos_sum = jnp.zeros((576, 256), f32)
         sin_sum = jnp.zeros((576, 256), f32)
@@ -381,7 +410,7 @@
                 packed[pl.ds(row + 144, 72), :] = jnp.where(low, pltpu.roll(first, 64, 1), second)
         return carry
 
-    lax.fori_loop(0, MMAX // 256, forward, 0)
+    lax.fori_loop(0, MMAX // 256, columns, 0)
 
     for i in range(ROWS):
         if i == ROWS - 1:
@@ -393,19 +422,14 @@
     ret_ref[...] = rows[...].astype(bf16)
 
 
-def cycle(scalars, weight, payload, m_row, table):
+def inverse(scalars, payload, m_row, table):
+    vmem = pl.BlockSpec(memory_space=pltpu.VMEM)
     return pl.pallas_call(
-        cycle_kernel,
-        in_specs=[
-            pl.BlockSpec(memory_space=pltpu.SMEM),
-            pl.BlockSpec(memory_space=pltpu.SMEM),
-            pl.BlockSpec(memory_space=pltpu.VMEM),
-            pl.BlockSpec(memory_space=pltpu.VMEM),
-            pl.BlockSpec(memory_space=pltpu.VMEM),
-        ],
-        out_specs=[pl.BlockSpec(memory_space=pltpu.VMEM)] * 3,
+        inverse_kernel,
+        in_specs=[pl.BlockSpec(memory_space=pltpu.SMEM), vmem, vmem, vmem],
+        out_specs=[vmem] * 3,
         out_shape=[
-            jax.ShapeDtypeStruct((128 * ROWS, 128), bf16),
+            jax.ShapeDtypeStruct((QUARTER // TILE, 576, TILE), bf16),
             jax.ShapeDtypeStruct((3, OUTR, 384), bf16),
             jax.ShapeDtypeStruct((3, OUTR, 384), bf16),
         ],
@@ -413,12 +437,33 @@
             pltpu.VMEM((128 * ROWS, 128), f32),
             pltpu.VMEM((128 * ROWS, 128), f32),
             pltpu.VMEM((576, 2 * MMAX), bf16),
-            pltpu.VMEM((QUARTER // TILE, 576, TILE), bf16),
             pltpu.VMEM((3, 5264, 128), f32),
         ],
-        compiler_params=params(56),
-        name="cycle",
-    )(scalars, weight, payload, m_row, table)
+        compiler_params=params(34),
+        cost_estimate=pl.CostEstimate(
+            flops=2 * QUARTER * 2 * MMAX * 576, bytes_accessed=12 << 20, transcendentals=0
+        ),
+        name="inverse",
+    )(scalars, payload, m_row, table)
+
+
+def forward(weight, m_row, table, flux):
+    vmem = pl.BlockSpec(memory_space=pltpu.VMEM)
+    return pl.pallas_call(
+        forward_kernel,
+        in_specs=[pl.BlockSpec(memory_space=pltpu.SMEM), vmem, vmem, vmem],
+        out_specs=vmem,
+        out_shape=jax.ShapeDtypeStruct((128 * ROWS, 128), bf16),
+        scratch_shapes=[
+            pltpu.VMEM((128 * ROWS, 128), f32),
+            pltpu.VMEM((128 * ROWS, 128), f32),
+        ],
+        compiler_params=params(20),
+        cost_estimate=pl.CostEstimate(
+            flops=2 * QUARTER * 2 * MMAX * 576, bytes_accessed=12 << 20, transcendentals=0
+        ),
+        name="forward",
+    )(weight, m_row, table, flux)
 
 
 def local(spectra, legendre, block_slot, wavenumber, cycle_points, quad_weight):
@@ -431,8 +476,9 @@
     m_row = wavenumber.reshape(WAVES, SLOTS).T.reshape(1, MMAX)
     table = tables(points, m_row)
     scalars = jnp.concatenate([points, lev[None].astype(jnp.int32)])
-    ret, keep, send = cycle(scalars, weight, received.reshape(128 * ROWS, 128), m_row, table)
+    flux, keep, send = inverse(scalars, received.reshape(128 * ROWS, 128), m_row, table)
     other = lax.ppermute(send, "lev", [(0, 1), (1, 0)])
+    ret = forward(weight, m_row, table, flux)
     returned = lax.all_to_all(
         ret.reshape(128, ROWS, 128), ("wave", "lev"), split_axis=0, concat_axis=0, tiled=True
     )

time: 119 us -> 106 us (0.89)
  waiting for transfers between devices: 27.2 us -> 22.5 us
  local copies, waits for them, and re-layouts: 14.6 us -> 11 us
  Pallas kernels: 55.4 us -> 52.3 us
  other arithmetic: 2.75 us -> 0.96 us
    ppermute x1, waiting for transfers between devices: 14.2 us -> 5.38 us  [local(): other = lax.ppermute(send, 'lev', [(0, 1), (1, 0)])]
    unnamed x20 -> x12, local copies, waits for them, and re-layouts: 10.1 us -> 6.59 us
    pallas_call x3 -> x4, Pallas kernels: 52.2 us -> 49.2 us  [the longest x1 16 us: analysis(): pl.pallas_call(analysis_kernel, in_specs=[pl.BlockSpec(memory_space=pltpu...]
    all_to_all x1, waiting for transfers between devices: 5.25 us -> 7.91 us  [local(): lax.all_to_all(ret.reshape(128, ROWS, 128), ('wave', 'lev'), split_axis=0...]
    all_to_all x1, waiting for transfers between devices: 7.76 us -> 9.19 us  [local(): lax.all_to_all(sent, ('wave', 'lev'), split_axis=0, concat_axis=0, tiled=...]
  transfers between devices with their start and end apart: 3 -> 3, of which waited for: 3 -> 3; matrix products, arithmetic and copies ran while one was open for 6% -> 5% of each run, Pallas kernels for 3% -> 11%
where the time goes in v2:
time: 106 us; the launch traced here: 105 us
  Pallas kernels  52.3 us (49%)
  waiting for transfers between devices  22.5 us (21%)
  starting transfers between devices  17.5 us (17%)
  local copies, waits for them, and re-layouts  11 us (10%)
    pallas_call x1, Pallas kernels, analysis(): pl.pallas_call(analysis_kernel, in_specs=[pl.BlockSpec(memory_space=pltpu...  16 us
    pallas_call x1, Pallas kernels, inverse(): pl.pallas_call(inverse_kernel, in_specs=[pl.BlockSpec(memory_space=pltpu....  12.6 us
    pallas_call x1, Pallas kernels, synthesis(): pl.pallas_call(synthesis_kernel, in_specs=[pl.BlockSpec(memory_space=pltp...  12.5 us
    all_to_all x1, starting transfers between devices, local(): lax.all_to_all(sent, ('wave', 'lev'), split_axis=0, concat_axis=0, tiled=...  11.5 us
    all_to_all x1, waiting for transfers between devices, local(): lax.all_to_all(sent, ('wave', 'lev'), split_axis=0, concat_axis=0, tiled=...  9.19 us
    pallas_call x1, Pallas kernels, forward(): pl.pallas_call(forward_kernel, in_specs=[pl.BlockSpec(memory_space=pltpu....  8.06 us
    all_to_all x1, waiting for transfers between devices, local(): lax.all_to_all(ret.reshape(128, ROWS, 128), ('wave', 'lev'), split_axis=0...  7.91 us
    unnamed x12, local copies, waits for them, and re-layouts  6.59 us
  transfers between devices with their start and end apart: 3, of which 3 were waited for; matrix products, arithmetic and copies ran while one was open for 5% of the time, Pallas kernels for 11%

profile of v2, /device:TPU:1, one launch (start us, length us, event | category | flops | bytes accessed | tf_op | source)
XLA Modules:
  0.0 105.2 jit_solution(3592826633921914148)
XLA Ops:
  0.6 0.0 copy-start.3
  0.6 0.0 copy-start.4
  0.6 12.5 %synthesis.1 = bf16[3072,128]{1,0:T(8,128)(2,1)} custom-call(s32[400]{0:T(512)} %slot_ref.3, bf16[6,400,1536]{2,1,0:T(8,128)(2,1)} %bitcast.15, bf16[400,64,128]{2,1,0:T(8,128)(2,1)} %leg_hbm.3), custom_call_target="tpu_custom_call" | custom-call | tf_op jit(solution)/shard_map/synthesis/pallas_call | solution.py:104
  13.1 11.5 %all-to-all-start = ((bf16[128,24,128]{2,1,0:T(8,128)(2,1)}), bf16[128,24,128]{2,1,0:T(8,128)(2,1)S(1)}, u32[]{:S(2)}, u32[]{:S(2)}) async-start(bf16[128,24,128]{2,1,0:T(8,128)(2,1)} %bitcast.18), calls=%async_computation | async-start | bytes 1572864 | tf_op jit(solution)/shard_map/all_to_all | solution.py:473
  24.6 0.0 copy-done.3
  24.7 0.1 reshape.25
  24.8 0.1 copy.9
  24.8 0.1 reshape.26.m_ref
  24.9 0.0 copy-done.4
  24.9 0.6 dynamic_slice.7.points_ref
  25.5 3.1 %tables.1.table_ref = bf16[1296,2560]{1,0:T(8,128)(2,1)S(1)} custom-call(s32[1]{0:T(128)} %dynamic_slice.7.points_ref, s32[1,1280]{1,0:T(1,128)S(1)} %reshape.26.m_ref), custom_call_target="tpu_custom_call" | custom-call | tf_op jit(solution)/shard_map/tables/pallas_call | solution.py:251
  28.7 0.0 copy-start
  28.7 2.8 %copy-done = bf16[1296,2560]{1,0:T(8,128)(2,1)} copy-done((bf16[1296,2560]{1,0:T(8,128)(2,1)}, bf16[1296,2560]{1,0:T(8,128)(2,1)S(1)}, u32[]{:S(2)}) %copy-start) | copy-done | bytes 6635544
  31.5 0.6 pad_add_fusion.scalar_ref
  32.1 9.2 %all-to-all-done = bf16[128,24,128]{2,1,0:T(8,128)(2,1)S(1)} async-done(((bf16[128,24,128]{2,1,0:T(8,128)(2,1)}), bf16[128,24,128]{2,1,0:T(8,128)(2,1)S(1)}, u32[]{:S(2)}, u32[]{:S(2)}) %all-to-all-start) | async-done | bytes 786464 | tf_op jit(solution)/shard_map/all_to_all | solution.py:473
  41.3 0.0 copy-start.1
  41.3 2.9 %copy-done.1 = bf16[1296,2560]{1,0:T(8,128)(2,1)S(1)} copy-done((bf16[1296,2560]{1,0:T(8,128)(2,1)S(1)}, bf16[1296,2560]{1,0:T(8,128)(2,1)}, u32[]{:S(2)}) %copy-start.1) | copy-done | bytes 6635544
  44.2 0.0 copy-start.5
  44.2 12.6 %inverse.1 = (bf16[3,576,432]{2,1,0:T(8,128)(2,1)S(1)}, bf16[3,336,384]{2,1,0:T(8,128)(2,1)S(1)}, bf16[3,336,384]{2,1,0:T(8,128)(2,1)S(1)}) custom-call(s32[2]{0:T(128)S(1)} %pad_add_fusion.scalar_ref, bf16[3072,128]{1,0:T(8,128)(2,1)S(1)} %bitcast.14, s32[1,1280]{1,0:T(1,128)S(1)} %reshape.26.m_ref, bf16[1296,2560]{1,0:T(8,128)(2,1)S(1)} %copy-done.1), custom_call_target="tpu_custom_call" | custom-call | flops 3822059520 | bytes 12582912 | tf_op jit(solution)/shard_map/inverse/pallas_call | solution.py:427
  56.8 0.9 collective-permute-start
  57.7 0.0 copy-done.5
  57.7 0.6 dynamic_slice.6.weight_ref
  58.3 8.1 %forward.1 = bf16[3072,128]{1,0:T(8,128)(2,1)} custom-call(f32[1]{0:T(128)} %dynamic_slice.6.weight_ref, s32[1,1280]{1,0:T(1,128)S(1)} %reshape.26.m_ref, bf16[1296,2560]{1,0:T(8,128)(2,1)S(1)} %copy-done.1, bf16[3,576,432]{2,1,0:T(8,128)(2,1)S(1)} %get-tuple-element.5.flux), custom_call_target="tpu_custom_call" | custom-call | flops 3822059520 | bytes 12582912 | tf_op jit(solution)/shard_map/forward/pallas_call | solution.py:452
  66.3 5.2 %all-to-all-start.1 = ((bf16[128,24,128]{2,1,0:T(8,128)(2,1)}), bf16[128,24,128]{2,1,0:T(8,128)(2,1)S(1)}, u32[]{:S(2)}, u32[]{:S(2)}) async-start(bf16[128,24,128]{2,1,0:T(8,128)(2,1)} %bitcast.5), calls=%async_computation.1 | async-start | bytes 1572864 | tf_op jit(solution)/shard_map/all_to_all | solution.py:482
  71.5 5.4 %collective-permute-done = bf16[3,336,384]{2,1,0:T(8,128)(2,1)S(1)} collective-permute-done((bf16[3,336,384]{2,1,0:T(8,128)(2,1)S(1)}, bf16[3,336,384]{2,1,0:T(8,128)(2,1)S(1)}, u32[]{:S(2)}, u32[]{:S(2)}) %collective-permute-start) | collective-permute-done | bytes 774176 | tf_op jit(solution)/shard_map/ppermute | solution.py:480
  76.9 0.1 select_bitcast_fusion.1
  77.0 0.2 pad_maximum_fusion
  77.2 0.2 copy.10
  77.4 2.9 %reshape.31 = bf16[2,3,123264]{2,0,1:T(2,128)(2,1)} reshape(bf16[2,3,321,384]{3,2,0,1:T(8,128)(2,1)S(1)} %copy.10) | data formatting | bytes 2958336 | tf_op jit(solution)/shard_map/reshape | solution.py:490
  80.2 7.9 %all-to-all-done.1 = bf16[128,24,128]{2,1,0:T(8,128)(2,1)S(1)} async-done(((bf16[128,24,128]{2,1,0:T(8,128)(2,1)}), bf16[128,24,128]{2,1,0:T(8,128)(2,1)S(1)}, u32[]{:S(2)}, u32[]{:S(2)}) %all-to-all-start.1) | async-done | bytes 786464 | tf_op jit(solution)/shard_map/all_to_all | solution.py:482
  88.2 0.9 copy-done.2
  89.0 16.0 %analysis.1 = bf16[6,400,1536]{2,1,0:T(8,128)(2,1)} custom-call(s32[400]{0:T(512)} %slot_ref.3, bf16[3072,128]{1,0:T(8,128)(2,1)} %bitcast.17, bf16[400,64,128]{2,1,0:T(8,128)(2,1)} %leg_hbm.3), custom_call_target="tpu_custom_call" | custom-call | tf_op jit(solution)/shard_map/analysis/pallas_call | solution.py:173
  (1 shorter events, 0.0 us)
Async XLA Ops:
  0.6 24.0 %copy-start.3 = (s32[1280]{0:T(1024)S(1)}, s32[1280]{0:T(1024)}, u32[]{:S(2)}) copy-start(s32[1280]{0:T(1024)} %param.9) | copy-start | bytes 15364
  0.6 24.3 %copy-start.4 = (s32[2]{0:T(128)S(1)}, s32[2]{0:T(128)}, u32[]{:S(2)}) copy-start(s32[2]{0:T(128)} %param.10) | copy-start | bytes 28
  13.1 28.2 %all-to-all-start = ((bf16[128,24,128]{2,1,0:T(8,128)(2,1)}), bf16[128,24,128]{2,1,0:T(8,128)(2,1)S(1)}, u32[]{:S(2)}, u32[]{:S(2)}) async-start(bf16[128,24,128]{2,1,0:T(8,128)(2,1)} %bitcast.18), calls=%async_computation | async-start | bytes 1572864 | tf_op jit(solution)/shard_map/all_to_all | solution.py:473
  28.7 2.8 %copy-start = (bf16[1296,2560]{1,0:T(8,128)(2,1)}, bf16[1296,2560]{1,0:T(8,128)(2,1)S(1)}, u32[]{:S(2)}) copy-start(bf16[1296,2560]{1,0:T(8,128)(2,1)S(1)} %tables.1.table_ref) | copy-start | bytes 19906564
  41.3 2.9 %copy-start.1 = (bf16[1296,2560]{1,0:T(8,128)(2,1)S(1)}, bf16[1296,2560]{1,0:T(8,128)(2,1)}, u32[]{:S(2)}) copy-start(bf16[1296,2560]{1,0:T(8,128)(2,1)} %copy-done) | copy-start | bytes 19906564
  44.2 13.5 %copy-start.5 = (f32[2]{0:T(128)S(1)}, f32[2]{0:T(128)}, u32[]{:S(2)}) copy-start(f32[2]{0:T(128)} %param.11) | copy-start | bytes 28
  56.8 20.1 %collective-permute-start = (bf16[3,336,384]{2,1,0:T(8,128)(2,1)S(1)}, bf16[3,336,384]{2,1,0:T(8,128)(2,1)S(1)}, u32[]{:S(2)}, u32[]{:S(2)}) collective-permute-start(bf16[3,336,384]{2,1,0:T(8,128)(2,1)S(1)} %get-tuple-element.7), channel_id=1, source_target_pairs={{0,1},{1,0},{2,3},{3,2},{4,5},{5,4},{6,7},{7,6},{8,9},{9,8},{10,11... | collective-permute-start | bytes 2322440 | tf_op jit(solution)/shard_map/ppermute | solution.py:480
  66.3 21.8 %all-to-all-start.1 = ((bf16[128,24,128]{2,1,0:T(8,128)(2,1)}), bf16[128,24,128]{2,1,0:T(8,128)(2,1)S(1)}, u32[]{:S(2)}, u32[]{:S(2)}) async-start(bf16[128,24,128]{2,1,0:T(8,128)(2,1)} %bitcast.5), calls=%async_computation.1 | async-start | bytes 1572864 | tf_op jit(solution)/shard_map/all_to_all | solution.py:482
  88.2 0.9 copy-start.2

commit v3 on v2

v3 whole, which is shorter than its diff:
```python
import functools
import math

import jax
import jax.numpy as jnp
from jax import lax
from jax.experimental import pallas as pl
from jax.experimental.pallas import tpu as pltpu
from jax.sharding import PartitionSpec as P

MMAX = 1280
NLON = 5136
NBLK = 64
WAVES = 64
SLOTS = 20
HALF = NLON // 2
PAYLOAD = 2880
ROWS = 24
QUARTER = 1408
FINE = 32
CHUNK = 256
OUTR = 336
GROUP = 16
RUNS = ((0, 32), (32, 96), (128, 96), (224, 96), (320, 80))
STRIDE = 73
FEW = 5

f32 = jnp.float32
bf16 = jnp.bfloat16


def params(mib):
    return pltpu.CompilerParams(vmem_limit_bytes=mib * 1024 * 1024)


def block_diagonal(block):
    zero = jnp.zeros_like(block)
    return jnp.concatenate(
        [jnp.concatenate([block, zero], axis=1), jnp.concatenate([zero, block], axis=1)], axis=0
    )


def copy_in(spec_hbm, leg_hbm, spec, leg, sems):
    copies = []
    for n, (first, count) in enumerate(RUNS):
        pair = [
            pltpu.make_async_copy(
                leg_hbm.at[pl.ds(first, count)], leg.at[pl.ds(first, count)], sems.at[0, n]
            )
        ]
        if spec is not None:
            pair.append(
                pltpu.make_async_copy(
                    spec_hbm.at[:, pl.ds(first, count)],
                    spec.at[:, pl.ds(first, count)],
                    sems.at[1, n],
                )
            )
        for copy in pair:
            copy.start()
        copies.append(pair)
    return copies


def synthesis_kernel(
    slot_ref, spec_hbm, leg_hbm, out_ref, order_ref, count_ref,
    spec, leg, sems, acc, stage, packed, rows,
):
    copies = copy_in(spec_hbm, leg_hbm, spec, leg, sems)
    acc[...] = jnp.zeros_like(acc)
    packed[...] = jnp.zeros_like(packed)
    for q in range(SLOTS + 1):
        count_ref[q] = 0

    def body(g, carry):
        base = pl.multiple_of(g * GROUP, GROUP)
        for c in range(6):
            x = spec[c, pl.ds(base, GROUP), :].astype(f32)
            for t in range(12):
                stage[pl.ds(c * 12 + t, GROUP, stride=STRIDE), :] = x[:, t * 128 : (t + 1) * 128]

        def product(kk):
            x = stage[kk * STRIDE : kk * STRIDE + 72, :].astype(bf16)
            return jnp.dot(x, block_diagonal(leg[base + kk]), preferred_element_type=f32)

        ahead = product(0)
        for kk in range(GROUP):
            prod = ahead
            if kk < GROUP - 1:
                ahead = product(kk + 1)
            slot = slot_ref[base + kk]
            acc[slot, 0:72, :] += prod[:, :128]
            acc[slot, 72:144, :] += prod[:, 128:]
            seen = count_ref[slot]
            count_ref[slot] = seen + 1
            order_ref[slot * 20 + seen] = base + kk
        return carry

    for (first, count), pair in zip(RUNS, copies):
        for copy in pair:
            copy.wait()
        lax.fori_loop(first // GROUP, (first + count) // GROUP, body, 0, unroll=True)

    for q in range(SLOTS):
        for r in range(2):
            for l2 in range(2):
                packed[pl.ds((q * 2 + r) * 72 + l2, 36, stride=2), :] = acc[
                    q, l2 * 72 + r * 36 : l2 * 72 + r * 36 + 36, :
                ]
    for i in range(ROWS):
        rows[pl.ds(i, 128, stride=ROWS), :] = packed[i * 128 : (i + 1) * 128, :].T
    out_ref[...] = rows[...].astype(bf16)


def synthesis(block_slot, spec, legendre):
    return pl.pallas_call(
        synthesis_kernel,
        in_specs=[
            pl.BlockSpec(memory_space=pltpu.SMEM),
            pl.BlockSpec(memory_space=pltpu.HBM),
            pl.BlockSpec(memory_space=pltpu.HBM),
        ],
        out_specs=[
            pl.BlockSpec(memory_space=pltpu.VMEM),
            pl.BlockSpec(memory_space=pltpu.SMEM),
            pl.BlockSpec(memory_space=pltpu.SMEM),
        ],
        scratch_shapes=[
            pltpu.VMEM(spec.shape, bf16),
            pltpu.VMEM(legendre.shape, bf16),
            pltpu.SemaphoreType.DMA((2, len(RUNS))),
            pltpu.VMEM((SLOTS + 1, 144, 128), f32),
            pltpu.VMEM((GROUP * 80, 128), f32),
            pltpu.VMEM((ROWS * 128, 128), f32),
            pltpu.VMEM((ROWS * 128, 128), f32),
        ],
        out_shape=[
            jax.ShapeDtypeStruct((128 * ROWS, 128), bf16),
            jax.ShapeDtypeStruct((SLOTS * 20 + legendre.shape[0],), jnp.int32),
            jax.ShapeDtypeStruct((SLOTS + 1,), jnp.int32),
        ],
        compiler_params=params(60),
        name="synthesis",
    )(block_slot, spec, legendre)


def block_at(order_ref, count, before, q, i):
    free = SLOTS * 20 + q * 20 + i - before - count
    return order_ref[jnp.where(i < count, q * 20 + i, free)]


def arrange_kernel(order_ref, count_ref, leg_hbm, out_hbm, leg, out_ref, sem, out_sems):
    copy = pltpu.make_async_copy(leg_hbm, leg, sem)
    copy.start()
    copy.wait()

    def slot_body(q, before):
        count = count_ref[q]
        for g in range(5):
            for e in range(0, 4, 2):
                first = block_at(order_ref, count, before, q, g * 4 + e)
                second = block_at(order_ref, count, before, q, g * 4 + e + 1)
                pair = jnp.concatenate([leg[first], leg[second]], axis=0)
                out_ref[q * 5 + g, :, e * 64 : e * 64 + 128] = pair.T
        return before + count

    before = 0
    written = []
    for n in range(SLOTS // FEW):
        before = lax.fori_loop(n * FEW, (n + 1) * FEW, slot_body, before, unroll=FEW)
        part = pl.ds(n * FEW * 5, FEW * 5)
        copy = pltpu.make_async_copy(out_ref.at[part], out_hbm.at[part], out_sems.at[n])
        copy.start()
        written.append(copy)
    for copy in written:
        copy.wait()


def arrange(order, counts, legendre):
    smem = pl.BlockSpec(memory_space=pltpu.SMEM)
    return pl.pallas_call(
        arrange_kernel,
        in_specs=[smem, smem, pl.BlockSpec(memory_space=pltpu.HBM)],
        out_specs=pl.BlockSpec(memory_space=pltpu.HBM),
        scratch_shapes=[
            pltpu.VMEM(legendre.shape, bf16),
            pltpu.VMEM((SLOTS * 5, 128, 256), bf16),
            pltpu.SemaphoreType.DMA(()),
            pltpu.SemaphoreType.DMA((SLOTS // FEW,)),
        ],
        out_shape=jax.ShapeDtypeStruct((SLOTS * 5, 128, 256), bf16),
        compiler_params=params(60),
        cost_estimate=pl.CostEstimate(flops=1 << 32, bytes_accessed=14 << 20, transcendentals=0),
        name="arrange",
    )(order, counts, legendre)


def analysis_kernel(
    order_ref, count_ref, in_ref, leg_hbm, out_hbm,
    leg_ref, out, in_sems, out_sems, coef, stage, packed, rows,
):
    copies = []
    for n in range(SLOTS // FEW):
        part = pl.ds(n * FEW * 5, FEW * 5)
        copy = pltpu.make_async_copy(leg_hbm.at[part], leg_ref.at[part], in_sems.at[n])
        copy.start()
        copies.append(copy)
    rows[...] = in_ref[...].astype(f32)
    for i in range(ROWS - 1):
        packed[i * 128 : (i + 1) * 128, :] = rows[pl.ds(i, 128, stride=ROWS), :].T
    for q in range(SLOTS):
        for l2 in range(2):
            for r in range(2):
                stage[l2 * 72 + r * 36 : l2 * 72 + r * 36 + 36, :] = packed[
                    pl.ds((q * 2 + r) * 72 + l2, 36, stride=2), :
                ]
        coef[q] = stage[0:144, :].astype(bf16)

    low = lax.broadcasted_iota(jnp.int32, (72, 128), 1) < 64

    def slot_body(q, before):
        lhs = coef[q]
        count = count_ref[q]
        ahead = jnp.dot(lhs, leg_ref[q * 5], preferred_element_type=f32)
        for g in range(5):
            value = ahead
            if g < 4:
                ahead = jnp.dot(lhs, leg_ref[q * 5 + g + 1], preferred_element_type=f32)
            for e in range(0, 4, 2):
                first = value[:72, e * 64 : e * 64 + 128]
                second = value[72:, e * 64 : e * 64 + 128]
                even = jnp.where(low, first, pltpu.roll(second, 64, 1))
                odd = jnp.where(low, pltpu.roll(first, 64, 1), second)
                for i, part in ((g * 4 + e, even), (g * 4 + e + 1, odd)):
                    k = block_at(order_ref, count, before, q, i)
                    stage[pl.ds(pl.multiple_of(k * 72, 8), 72), :] = jnp.where(
                        i < count, part, 0.0
                    )
        return before + count

    before = 0
    for n in range(SLOTS // FEW):
        copies[n].wait()
        before = lax.fori_loop(n * FEW, (n + 1) * FEW, slot_body, before, unroll=FEW)

    def body(g, carry):
        base = pl.multiple_of(g * GROUP, GROUP)
        for c in range(6):
            for t in range(12):
                out[c, pl.ds(base, GROUP), t * 128 : (t + 1) * 128] = stage[
                    pl.ds(pl.multiple_of(base * 72, 8) + c * 12 + t, GROUP, stride=72), :
                ].astype(bf16)
        return carry

    written = []
    for n, (first, count) in enumerate(RUNS):
        lax.fori_loop(first // GROUP, (first + count) // GROUP, body, 0)
        copy = pltpu.make_async_copy(
            out.at[:, pl.ds(first, count)], out_hbm.at[:, pl.ds(first, count)], out_sems.at[n]
        )
        copy.start()
        written.append(copy)
    for copy in written:
        copy.wait()


def analysis(order, counts, payload, arranged, blocks):
    shape = (6, blocks, 24 * NBLK)
    return pl.pallas_call(
        analysis_kernel,
        in_specs=[
            pl.BlockSpec(memory_space=pltpu.SMEM),
            pl.BlockSpec(memory_space=pltpu.SMEM),
            pl.BlockSpec(memory_space=pltpu.VMEM),
            pl.BlockSpec(memory_space=pltpu.HBM),
        ],
        out_specs=pl.BlockSpec(memory_space=pltpu.HBM),
        scratch_shapes=[
            pltpu.VMEM(arranged.shape, bf16),
            pltpu.VMEM(shape, bf16),
            pltpu.SemaphoreType.DMA((SLOTS // FEW,)),
            pltpu.SemaphoreType.DMA((len(RUNS),)),
            pltpu.VMEM((SLOTS, 144, 128), bf16),
            pltpu.VMEM((blocks * 72, 128), f32),
            pltpu.VMEM((ROWS * 128, 128), f32),
            pltpu.VMEM((ROWS * 128, 128), f32),
        ],
        out_shape=jax.ShapeDtypeStruct(shape, bf16),
        compiler_params=params(48),
        name="analysis",
    )(order, counts, payload, arranged)


def cosine_sine(phase, points, inverse):
    turns = jnp.floor(phase * inverse + 0.5)
    rest = phase - turns * points
    quarter = jnp.floor(4.0 * rest * inverse + 0.5)
    z = (4.0 * rest - quarter * points) * inverse * (0.5 * math.pi)
    z2 = z * z
    s = z * (1.0 + z2 * (-1 / 6 + z2 * (1 / 120 + z2 * (-1 / 5040 + z2 * (1 / 362880)))))
    c = 1.0 + z2 * (-0.5 + z2 * (1 / 24 + z2 * (-1 / 720 + z2 * (1 / 40320))))
    odd = jnp.abs(quarter) == 1.0
    flip = jnp.abs(quarter) == 2.0
    first = jnp.where(odd, s, c)
    second = jnp.where(odd, c, s)
    cos_sign = jnp.where(flip | (quarter == 1.0), -1.0, 1.0)
    sin_sign = jnp.where(flip | (quarter == -1.0), -1.0, 1.0)
    return first * cos_sign, second * sin_sign


def table_kernel(
    points_ref, m_ref, out_hbm, flip_hbm,
    out_ref, flip_ref, sems, fine_c, fine_s, coarse_c, coarse_s, column, turn_c, turn_s,
):
    count = points_ref[lax.axis_index("lev")]
    points = jnp.full((1, MMAX), count, jnp.int32).astype(f32)
    inverse = 1.0 / points
    m = m_ref[...].astype(f32)
    live = jnp.where(2.0 * m < points, 1.0, 0.0)
    for base in range(0, FINE, 8):
        index = (base + lax.broadcasted_iota(jnp.int32, (8, MMAX), 0)).astype(f32)
        c, s = cosine_sine(index * m, points, inverse)
        fine_c[base : base + 8, :] = c
        fine_s[base : base + 8, :] = s
    for base in range(0, coarse_c.shape[0], 8):
        index = (FINE * (base + lax.broadcasted_iota(jnp.int32, (8, MMAX), 0))).astype(f32)
        c, s = cosine_sine(index * m, points, inverse)
        coarse_c[base : base + 8, :] = c * live
        coarse_s[base : base + 8, :] = s * live

    def row_body(row, carry):
        rows = pl.ds(pl.multiple_of(row * FINE, FINE), FINE)
        for n in range(MMAX // CHUNK):
            at = slice(n * CHUNK, (n + 1) * CHUNK)
            cb = coarse_c[pl.ds(row, 1), at]
            sb = coarse_s[pl.ds(row, 1), at]
            cf = fine_c[:, at]
            sf = fine_s[:, at]
            out_ref[n, 0, rows, :] = (cb * cf - sb * sf).astype(bf16)
            out_ref[n, 1, rows, :] = (-(sb * cf + cb * sf)).astype(bf16)
        return carry

    written = []

    def write(source, target, n):
        copy = pltpu.make_async_copy(source, target, sems.at[n])
        copy.start()
        written.append(copy)

    few = QUARTER // FINE // 4
    for n in range(4):
        lax.fori_loop(n * few, (n + 1) * few, row_body, 0)
        part = pl.ds(n * few * FINE, few * FINE)
        write(out_ref.at[:, :, part], out_hbm.at[:, :, part], n)

    whole_c, whole_s = cosine_sine(128.0 * m, points, inverse)
    for n in range(MMAX // 128):
        at = slice(n * 128, (n + 1) * 128)
        for row, target in ((m, column), (whole_c, turn_c), (whole_s, turn_s)):
            target[at, :] = jnp.broadcast_to(row[:, at], (128, 128)).T
    points_row = points[:, :128]
    inverse_row = inverse[:, :128]
    lane = lax.broadcasted_iota(jnp.int32, (32, 128), 1).astype(f32)

    def column_body(g, carry):
        at = pl.multiple_of(g * 32, 32)
        mc = column[pl.ds(at, 32), :]
        alive = jnp.where(2.0 * mc < points_row, 1.0, 0.0)
        c, s = cosine_sine(lane * mc, points_row, inverse_row)
        c, s = c * alive, s * alive
        tc, ts = turn_c[pl.ds(at, 32), :], turn_s[pl.ds(at, 32), :]
        for a in range(QUARTER // 128):
            flip_ref[pl.ds(at, 32), a * 128 : (a + 1) * 128] = c.astype(bf16)
            flip_ref[pl.ds(MMAX + at, 32), a * 128 : (a + 1) * 128] = (-s).astype(bf16)
            c, s = c * tc - s * ts, s * tc + c * ts
        return carry

    for n in range(4):
        lax.fori_loop(n * 10, (n + 1) * 10, column_body, 0, unroll=2)
        for r in range(2):
            part = pl.ds(r * MMAX + n * 320, 320)
            write(flip_ref.at[part], flip_hbm.at[part], 4 + 2 * n + r)
    for copy in written:
        copy.wait()


def tables(points, m_row):
    vmem = pl.BlockSpec(memory_space=pltpu.VMEM)
    return pl.pallas_call(
        table_kernel,
        in_specs=[pl.BlockSpec(memory_space=pltpu.SMEM), vmem],
        out_specs=[pl.BlockSpec(memory_space=pltpu.HBM)] * 2,
        scratch_shapes=[
            pltpu.VMEM((MMAX // CHUNK, 2, QUARTER, CHUNK), bf16),
            pltpu.VMEM((2 * MMAX, QUARTER), bf16),
            pltpu.SemaphoreType.DMA((12,)),
            pltpu.VMEM((FINE, MMAX), f32),
            pltpu.VMEM((FINE, MMAX), f32),
            pltpu.VMEM((48, MMAX), f32),
            pltpu.VMEM((48, MMAX), f32),
            pltpu.VMEM((MMAX, 128), f32),
            pltpu.VMEM((MMAX, 128), f32),
            pltpu.VMEM((MMAX, 128), f32),
        ],
        out_shape=[
            jax.ShapeDtypeStruct((MMAX // CHUNK, 2, QUARTER, CHUNK), bf16),
            jax.ShapeDtypeStruct((2 * MMAX, QUARTER), bf16),
        ],
        compiler_params=params(60),
        name="tables",
    )(points, m_row)


def rotation(m):
    k = m & 3
    a = jnp.where(k == 0, 1.0, jnp.where(k == 2, -1.0, 0.0))
    b = jnp.where(k == 1, 1.0, jnp.where(k == 3, -1.0, 0.0))
    sign = jnp.where((k & 1) == 0, 1.0, -1.0)
    return a.astype(f32), b.astype(f32), sign.astype(f32)


def unpack_kernel(in_ref, m_ref, coef, rows, packed):
    low = lax.broadcasted_iota(jnp.int32, (72, 128), 1) < 64

    rows[...] = in_ref[...].astype(f32)
    for i in range(ROWS - 1):
        block = jnp.concatenate(
            [
                rows[pl.ds(i, WAVES, stride=2 * ROWS), :],
                rows[pl.ds(ROWS + i, WAVES, stride=2 * ROWS), :],
            ],
            axis=0,
        )
        packed[i * 128 : (i + 1) * 128, :] = block.T

    for i in range(SLOTS // 2):
        lanes = slice(i * 128, (i + 1) * 128)
        m = m_ref[:, lanes]
        factor = jnp.where(m == 0, 1.0, 2.0).astype(f32)
        a, b, sign = rotation(m)
        parts = []
        for r in range(2):
            even = packed[(4 * i + r) * 72 : (4 * i + r + 1) * 72, :]
            odd = packed[(4 * i + 2 + r) * 72 : (4 * i + 3 + r) * 72, :]
            first = jnp.where(low, even, pltpu.roll(odd, 64, 1)) * factor
            second = jnp.where(low, pltpu.roll(even, 64, 1), odd) * factor
            parts.append((first, second))
        (re0, re1), (im0, im1) = parts
        for f in range(3):
            at = slice(f * 24, (f + 1) * 24)
            re = jnp.concatenate([re0[at], re1[at]], axis=0)
            im = jnp.concatenate([im0[at], im1[at]], axis=0)
            turned = [
                (re, im),
                (a * re - b * im, a * im + b * re),
                (sign * re, sign * im),
                (a * re + b * im, a * im - b * re),
            ]
            for r4 in range(4):
                out = slice(f * 192 + r4 * 48, f * 192 + (r4 + 1) * 48)
                coef[out, i * 128 : (i + 1) * 128] = turned[r4][0].astype(bf16)
                coef[out, MMAX + i * 128 : MMAX + (i + 1) * 128] = turned[r4][1].astype(bf16)


def inverse_kernel(points_ref, coef, flip, flux, keep_ref, send_ref, grid):
    lev = lax.axis_index("lev")
    points = points_ref[lev]
    quarter = points >> 2

    def transform(start, size):
        values = jnp.dot(
            coef[...], flip[:, pl.ds(start, size)], preferred_element_type=f32
        )
        index = start + lax.broadcasted_iota(jnp.int32, (192, size), 1)
        fields = [
            jnp.where(index < quarter, values[f * 192 : (f + 1) * 192], 0.0)
            .astype(bf16)
            .astype(f32)
            for f in range(3)
        ]
        products = [fields[0] * fields[2], fields[1] * fields[2], 0.5 * fields[2] * fields[2]]
        for f in range(3):
            flux[f * 192 : (f + 1) * 192, pl.ds(start, size)] = products[f].astype(bf16)
        for f in range(3):
            for r4 in range(4):
                grid[f, pl.ds(r4 * quarter + start, size), 0:48] = fields[f][
                    r4 * 48 : (r4 + 1) * 48
                ].T

    transform(QUARTER - 128, 128)

    def tile(step, carry):
        transform(pl.multiple_of((QUARTER // CHUNK - 1 - step) * CHUNK, CHUNK), CHUNK)
        return carry

    lax.fori_loop(0, QUARTER // CHUNK, tile, 0, unroll=5)

    chunk = 48
    for which, ref in ((0, keep_ref), (1, send_ref)):
        half = lev if which == 0 else 1 - lev

        def place(j, carry, half=half, ref=ref):
            lines = []
            for f in range(3):
                pieces = []
                for s in range(8):
                    first = half * HALF + j * (8 * chunk) + s
                    piece = grid[f, pl.ds(first, chunk, stride=8), :][:, 0:48]
                    place_of = first + 8 * lax.broadcasted_iota(jnp.int32, (chunk, 48), 0)
                    pieces.append(jnp.where(place_of < points, piece, 0.0))
                lines.append(jnp.concatenate(pieces, axis=1).astype(bf16))
            for f in range(3):
                ref[f, pl.ds(pl.multiple_of(j * chunk, 16), chunk), :] = lines[f]
            return carry

        lax.fori_loop(0, OUTR // chunk, place, 0, unroll=7)


def forward_kernel(weight_ref, m_ref, table, flux, ret_ref, rows, packed):
    low = lax.broadcasted_iota(jnp.int32, (72, 128), 1) < 64
    weight = weight_ref[lax.axis_index("lev")]

    for n in range(MMAX // CHUNK):
        at = n * CHUNK
        cos_sum = jnp.dot(flux[...], table[n, 0], preferred_element_type=f32)
        sin_sum = jnp.dot(flux[...], table[n, 1], preferred_element_type=f32)
        for i2 in range(2):
            lanes = slice(i2 * 128, (i2 + 1) * 128)
            a, b, sign = rotation(m_ref[:, pl.ds(at + i2 * 128, 128)])
            result = [[], []]
            for f in range(3):
                c = [cos_sum[f * 192 + r4 * 48 : f * 192 + (r4 + 1) * 48, lanes] for r4 in range(4)]
                s = [sin_sum[f * 192 + r4 * 48 : f * 192 + (r4 + 1) * 48, lanes] for r4 in range(4)]
                result[0].append(
                    (c[0] + sign * c[2] + a * (c[1] + c[3]) + b * (s[1] - s[3])) * weight
                )
                result[1].append(
                    (s[0] + sign * s[2] + a * (s[1] + s[3]) - b * (c[1] - c[3])) * weight
                )
            for r in range(2):
                first = jnp.concatenate([x[:24] for x in result[r]], axis=0)
                second = jnp.concatenate([x[24:] for x in result[r]], axis=0)
                row = (n * 8 + 4 * i2 + r) * 72
                packed[pl.ds(row, 72), :] = jnp.where(low, first, pltpu.roll(second, 64, 1))
                packed[pl.ds(row + 144, 72), :] = jnp.where(low, pltpu.roll(first, 64, 1), second)

    for i in range(ROWS):
        if i == ROWS - 1:
            block = jnp.zeros((128, 128), f32)
        else:
            block = packed[i * 128 : (i + 1) * 128, :].T
        rows[pl.ds(i, WAVES, stride=2 * ROWS), :] = block[:64]
        rows[pl.ds(ROWS + i, WAVES, stride=2 * ROWS), :] = block[64:]
    ret_ref[...] = rows[...].astype(bf16)


def unpack(payload, m_row):
    vmem = pl.BlockSpec(memory_space=pltpu.VMEM)
    return pl.pallas_call(
        unpack_kernel,
        in_specs=[vmem, vmem],
        out_specs=vmem,
        out_shape=jax.ShapeDtypeStruct((576, 2 * MMAX), bf16),
        scratch_shapes=[
            pltpu.VMEM((128 * ROWS, 128), f32),
            pltpu.VMEM((128 * ROWS, 128), f32),
        ],
        compiler_params=params(16),
        cost_estimate=pl.CostEstimate(flops=1 << 33, bytes_accessed=1 << 20, transcendentals=0),
        name="unpack",
    )(payload, m_row)


def inverse(points, coef, flip):
    vmem = pl.BlockSpec(memory_space=pltpu.VMEM)
    return pl.pallas_call(
        inverse_kernel,
        in_specs=[pl.BlockSpec(memory_space=pltpu.SMEM), vmem, vmem],
        out_specs=[vmem] * 3,
        out_shape=[
            jax.ShapeDtypeStruct((576, QUARTER), bf16),
            jax.ShapeDtypeStruct((3, OUTR, 384), bf16),
            jax.ShapeDtypeStruct((3, OUTR, 384), bf16),
        ],
        scratch_shapes=[pltpu.VMEM((3, 5264, 128), f32)],
        compiler_params=params(20),
        cost_estimate=pl.CostEstimate(
            flops=2 * QUARTER * 2 * MMAX * 576, bytes_accessed=12 << 20, transcendentals=0
        ),
        name="inverse",
    )(points, coef, flip)


def forward(weight, m_row, table, flux):
    vmem = pl.BlockSpec(memory_space=pltpu.VMEM)
    return pl.pallas_call(
        forward_kernel,
        in_specs=[
            pl.BlockSpec(memory_space=pltpu.SMEM), vmem, vmem, vmem
        ],
        out_specs=vmem,
        out_shape=jax.ShapeDtypeStruct((128 * ROWS, 128), bf16),
        scratch_shapes=[
            pltpu.VMEM((128 * ROWS, 128), f32),
            pltpu.VMEM((128 * ROWS, 128), f32),
        ],
        compiler_params=params(20),
        cost_estimate=pl.CostEstimate(
            flops=2 * QUARTER * 2 * MMAX * 576, bytes_accessed=12 << 20, transcendentals=0
        ),
        name="forward",
    )(weight, m_row, table, flux)


def local(spectra, legendre, block_slot, wavenumber, cycle_points, quad_weight):
    lev = lax.axis_index("lev")
    spec = jnp.transpose(spectra, (1, 0, 2))
    sent, order, counts = synthesis(block_slot, spec, legendre)
    sent = sent.reshape(128, ROWS, 128)
    received = lax.all_to_all(sent, ("wave", "lev"), split_axis=0, concat_axis=0, tiled=True)
    m_row = wavenumber.reshape(WAVES, SLOTS).T.reshape(1, MMAX)
    table, flip = tables(cycle_points, m_row)
    coef = unpack(received.reshape(128 * ROWS, 128), m_row)
    flux, keep, send = inverse(cycle_points, coef, flip)
    other = lax.ppermute(send, "lev", [(0, 1), (1, 0)])
    ret = forward(quad_weight, m_row, table, flux)
    returned = lax.all_to_all(
        ret.reshape(128, ROWS, 128), ("wave", "lev"), split_axis=0, concat_axis=0, tiled=True
    )
    arranged = arrange(order, counts, legendre)
    tendency = analysis(
        order, counts, returned.reshape(128 * ROWS, 128), arranged, legendre.shape[0]
    )
    own_first = lev == 0
    both = jnp.stack(
        [jnp.where(own_first, keep, other), jnp.where(own_first, other, keep)], axis=0
    )
    grid_fields = both[:, :, : HALF // 8, :].reshape(2, 3, HALF * 48)
    return (jnp.transpose(tendency, (1, 0, 2)), grid_fields)


def solution(mesh):
    placed = (P("wave", None, "lev"), P("wave", None, None), P("wave"), P(), P("wave"), P("wave"))
    return jax.shard_map(
        local,
        mesh=mesh,
        in_specs=placed,
        out_specs=(P("wave", None, "lev"), P("wave", None, "lev")),
        check_vma=False,
    )
```

time: 106 us -> 91.8 us (0.87)
  waiting for transfers between devices: 22.5 us -> 13.5 us
  local copies, waits for them, and re-layouts: 11 us -> 6.4 us
    pallas_call x1 -> x3, Pallas kernels: 3.13 us -> 17.3 us  [the longest x1 9.22 us: tables(): pl.pallas_call(table_kernel, in_specs=[pl.BlockSpec(memory_space=pltpu.SM...]
    pallas_call x1, Pallas kernels: 16 us -> 11 us  [analysis(): pl.pallas_call(analysis_kernel, in_specs=[pl.BlockSpec(memory_space=pltpu...]
    ppermute x1, waiting for transfers between devices: 5.38 us -> 0.65 us  [local(): other = lax.ppermute(send, 'lev', [(0, 1), (1, 0)])]
    pallas_call x1, Pallas kernels: 12.6 us -> 7.96 us  [inverse(): pl.pallas_call(inverse_kernel, in_specs=[pl.BlockSpec(memory_space=pltpu....]
    unnamed x12 -> x18, local copies, waits for them, and re-layouts: 6.59 us -> 2.53 us
    pallas_call x1, Pallas kernels: 12.5 us -> 9.66 us  [synthesis(): pl.pallas_call(synthesis_kernel, in_specs=[pl.BlockSpec(memory_space=pltp...]
    all_to_all x1, waiting for transfers between devices: 9.19 us -> 6.53 us  [local(): lax.all_to_all(sent, ('wave', 'lev'), split_axis=0, concat_axis=0, tiled=...]
    all_to_all x1, waiting for transfers between devices: 7.91 us -> 6.33 us  [local(): lax.all_to_all(ret.reshape(128, ROWS, 128), ('wave', 'lev'), split_axis=0...]
  transfers between devices with their start and end apart: 3 -> 3, of which waited for: 3 -> 3; matrix products, arithmetic and copies ran while one was open for 5% -> 5% of each run, Pallas kernels for 11% -> 25%
where the time goes in v3:
time: 91.8 us; the launch traced here: 91.4 us
  Pallas kernels  52.4 us (57%)
  starting transfers between devices  17.8 us (19%)
  waiting for transfers between devices  13.5 us (15%)
  local copies, waits for them, and re-layouts  6.4 us (7%)
  between operations  0.94 us (1%)
    all_to_all x1, starting transfers between devices, local(): lax.all_to_all(sent, ('wave', 'lev'), split_axis=0, concat_axis=0, tiled=...  11.5 us
    pallas_call x1, Pallas kernels, analysis(): pl.pallas_call(analysis_kernel, in_specs=[pl.BlockSpec(memory_space=pltpu...  11 us
    pallas_call x1, Pallas kernels, synthesis(): pl.pallas_call(synthesis_kernel, in_specs=[pl.BlockSpec(memory_space=pltp...  9.66 us
    pallas_call x1, Pallas kernels, tables(): pl.pallas_call(table_kernel, in_specs=[pl.BlockSpec(memory_space=pltpu.SM...  9.22 us
    pallas_call x1, Pallas kernels, inverse(): pl.pallas_call(inverse_kernel, in_specs=[pl.BlockSpec(memory_space=pltpu....  7.96 us
    pallas_call x1, Pallas kernels, arrange(): pl.pallas_call(arrange_kernel, in_specs=[smem, smem, pl.BlockSpec(memory_...  6.81 us
    pallas_call x1, Pallas kernels, forward(): pl.pallas_call(forward_kernel, in_specs=[pl.BlockSpec(memory_space=pltpu....  6.54 us
    all_to_all x1, waiting for transfers between devices, local(): lax.all_to_all(sent, ('wave', 'lev'), split_axis=0, concat_axis=0, tiled=...  6.53 us
  transfers between devices with their start and end apart: 3, of which 3 were waited for; matrix products, arithmetic and copies ran while one was open for 5% of the time, Pallas kernels for 25%

profile of v3, /device:TPU:1, one launch (start us, length us, event | category | flops | bytes accessed | tf_op | source)
XLA Modules:
  0.0 91.4 jit_solution(13561941194853257131)
XLA Ops:
  0.6 0.0 copy-start.8
  0.6 9.7 %synthesis.1 = (bf16[3072,128]{1,0:T(8,128)(2,1)}, s32[800]{0:T(1024)}, s32[21]{0:T(128)}) custom-call(s32[400]{0:T(512)} %slot_ref.1, bf16[6,400,1536]{2,1,0:T(8,128)(2,1)} %bitcast.16, bf16[400,64,128]{2,1,0:T(8,128)(2,1)} %leg_hbm.3), custom_call_target="tpu_custom_call" | custom-call | tf_op jit(solution)/shard_map/synthesis/pallas_call | solution.py:116
  10.3 11.5 %all-to-all-start = ((bf16[128,24,128]{2,1,0:T(8,128)(2,1)}), bf16[128,24,128]{2,1,0:T(8,128)(2,1)S(1)}, u32[]{:S(2)}, u32[]{:S(2)}) async-start(bf16[128,24,128]{2,1,0:T(8,128)(2,1)} %bitcast.17), calls=%async_computation | async-start | bytes 1572864 | tf_op jit(solution)/shard_map/all_to_all | solution.py:620
  21.8 0.0 copy-done.8
  21.9 0.1 reshape.25
  22.0 0.1 copy.9
  22.0 0.7 reshape.26.m_ref
  22.7 9.2 %tables.1 = (bf16[5,2,1408,256]{3,2,1,0:T(8,128)(2,1)}, bf16[2560,1408]{1,0:T(8,128)(2,1)}) custom-call(s32[2]{0:T(128)} %points_ref.3, s32[1,1280]{1,0:T(1,128)} %reshape.26.m_ref), custom_call_target="tpu_custom_call" | custom-call | tf_op jit(solution)/shard_map/tables/pallas_call | solution.py:389
  32.0 6.5 %all-to-all-done = bf16[128,24,128]{2,1,0:T(8,128)(2,1)S(1)} async-done(((bf16[128,24,128]{2,1,0:T(8,128)(2,1)}), bf16[128,24,128]{2,1,0:T(8,128)(2,1)S(1)}, u32[]{:S(2)}, u32[]{:S(2)}) %all-to-all-start) | async-done | bytes 786464 | tf_op jit(solution)/shard_map/all_to_all | solution.py:620
  38.5 0.7 copy-done
  39.2 1.2 %unpack.1.coef = bf16[576,2560]{1,0:T(8,128)(2,1)S(1)} custom-call(bf16[3072,128]{1,0:T(8,128)(2,1)S(1)} %bitcast.14, s32[1,1280]{1,0:T(1,128)S(1)} %copy-done), custom_call_target="tpu_custom_call" | custom-call | flops 8589934592 | bytes 1048576 | tf_op jit(solution)/shard_map/unpack/pallas_call | solution.py:559
  40.4 0.0 copy-done.4
  40.4 1.8 %copy-done.6 = bf16[2560,1408]{1,0:T(8,128)(2,1)S(1)} copy-done((bf16[2560,1408]{1,0:T(8,128)(2,1)S(1)}, bf16[2560,1408]{1,0:T(8,128)(2,1)}, u32[]{:S(2)}) %copy-start.6) | copy-done | bytes 7208984
  42.2 8.0 %inverse.1 = (bf16[576,1408]{1,0:T(8,128)(2,1)S(1)}, bf16[3,336,384]{2,1,0:T(8,128)(2,1)S(1)}, bf16[3,336,384]{2,1,0:T(8,128)(2,1)S(1)}) custom-call(s32[2]{0:T(128)S(1)} %copy-done.4, bf16[576,2560]{1,0:T(8,128)(2,1)S(1)} %unpack.1.coef, bf16[2560,1408]{1,0:T(8,128)(2,1)S(1)} %copy-done.6), custom_call_target="tpu_custom_call" | custom-call | flops 4152360960 | bytes 12582912 | tf_op jit(solution)/shard_map/inverse/pallas_call | solution.py:576
  50.2 1.1 %collective-permute-start = (bf16[3,336,384]{2,1,0:T(8,128)(2,1)S(1)}, bf16[3,336,384]{2,1,0:T(8,128)(2,1)S(1)}, u32[]{:S(2)}, u32[]{:S(2)}) collective-permute-start(bf16[3,336,384]{2,1,0:T(8,128)(2,1)S(1)} %get-tuple-element.17), channel_id=1, source_target_pairs={{0,1},{1,0},{2,3},{3,2},{4,5},{5,4},{6,7},{7,6},{8,9},{9,8},{10,11... | collective-permute-start | bytes 2322440 | tf_op jit(solution)/shard_map/ppermute | solution.py:625
  51.3 0.0 copy-done.1
  51.3 0.0 copy-done.5
  51.3 0.0 copy-done.7
  51.3 6.5 %forward.1 = bf16[3072,128]{1,0:T(8,128)(2,1)} custom-call(f32[2]{0:T(128)S(1)} %copy-done.7, s32[1,1280]{1,0:T(1,128)S(1)} %copy-done.1, bf16[5,2,1408,256]{3,2,1,0:T(8,128)(2,1)S(1)} %copy-done.5, bf16[576,1408]{1,0:T(8,128)(2,1)S(1)} %get-tuple-element.15.flux), custom_call_target="tpu_custom_call" | custom-call | flops 4152360960 | bytes 12582912 | tf_op jit(solution)/shard_map/forward/pallas_call | solution.py:596
  57.9 5.2 %all-to-all-start.1 = ((bf16[128,24,128]{2,1,0:T(8,128)(2,1)}), bf16[128,24,128]{2,1,0:T(8,128)(2,1)S(1)}, u32[]{:S(2)}, u32[]{:S(2)}) async-start(bf16[128,24,128]{2,1,0:T(8,128)(2,1)} %bitcast.4), calls=%async_computation.1 | async-start | bytes 1572864 | tf_op jit(solution)/shard_map/all_to_all | solution.py:627
  63.0 6.8 %arrange.1.leg_hbm = bf16[100,128,256]{2,1,0:T(8,128)(2,1)} custom-call(s32[800]{0:T(1024)} %get-tuple-element.10.order_ref, s32[21]{0:T(128)} %get-tuple-element.11.count_ref, bf16[400,64,128]{2,1,0:T(8,128)(2,1)} %leg_hbm.3), custom_call_target="tpu_custom_call" | custom-call | flops 4294967296 | bytes 14680064 | tf_op jit(solution)/shard_map/arrange/pallas_call | solution.py:181
  69.8 0.7 collective-permute-done
  70.5 0.1 select_bitcast_fusion.1
  70.6 0.2 pad_maximum_fusion
  70.8 0.0 copy-start.2
  70.8 0.0 copy-start.3
  70.8 0.2 copy.10
  71.0 2.9 %reshape.31 = bf16[2,3,123264]{2,0,1:T(2,128)(2,1)} reshape(bf16[2,3,321,384]{3,2,0,1:T(8,128)(2,1)S(1)} %copy.10) | data formatting | bytes 2958336 | tf_op jit(solution)/shard_map/reshape | solution.py:638
  73.9 6.3 %all-to-all-done.1 = bf16[128,24,128]{2,1,0:T(8,128)(2,1)S(1)} async-done(((bf16[128,24,128]{2,1,0:T(8,128)(2,1)}), bf16[128,24,128]{2,1,0:T(8,128)(2,1)S(1)}, u32[]{:S(2)}, u32[]{:S(2)}) %all-to-all-start.1) | async-done | bytes 786464 | tf_op jit(solution)/shard_map/all_to_all | solution.py:627
  80.2 0.0 copy-done.2
  80.2 0.0 copy-done.3
  80.2 11.0 %analysis.1 = bf16[6,400,1536]{2,1,0:T(8,128)(2,1)} custom-call(s32[800]{0:T(1024)S(1)} %copy-done.2, s32[21]{0:T(128)S(1)} %copy-done.3, bf16[3072,128]{1,0:T(8,128)(2,1)S(1)} %bitcast.13, bf16[100,128,256]{2,1,0:T(8,128)(2,1)} %arrange.1.leg_hbm), custom_call_target="tpu_custom_call" | custom-call | tf_op jit(solution)/shard_map/analysis/pallas_call | solution.py:269
  (6 shorter events, 0.0 us)
Async XLA Ops:
  0.6 21.2 %copy-start.8 = (s32[1280]{0:T(1024)S(1)}, s32[1280]{0:T(1024)}, u32[]{:S(2)}) copy-start(s32[1280]{0:T(1024)} %param.9) | copy-start | bytes 15364
  10.3 28.2 %all-to-all-start = ((bf16[128,24,128]{2,1,0:T(8,128)(2,1)}), bf16[128,24,128]{2,1,0:T(8,128)(2,1)S(1)}, u32[]{:S(2)}, u32[]{:S(2)}) async-start(bf16[128,24,128]{2,1,0:T(8,128)(2,1)} %bitcast.17), calls=%async_computation | async-start | bytes 1572864 | tf_op jit(solution)/shard_map/all_to_all | solution.py:620
  38.5 0.7 copy-start
  39.2 1.2 %copy-start.4 = (s32[2]{0:T(128)S(1)}, s32[2]{0:T(128)}, u32[]{:S(2)}) copy-start(s32[2]{0:T(128)} %points_ref.3) | copy-start | bytes 28
  39.2 3.1 %copy-start.6 = (bf16[2560,1408]{1,0:T(8,128)(2,1)S(1)}, bf16[2560,1408]{1,0:T(8,128)(2,1)}, u32[]{:S(2)}) copy-start(bf16[2560,1408]{1,0:T(8,128)(2,1)} %get-tuple-element.14.flip) | copy-start | bytes 21626884
  42.2 9.1 %copy-start.1 = (s32[1,1280]{1,0:T(1,128)S(1)}, s32[1,1280]{1,0:T(1,128)}, u32[]{:S(2)}) copy-start(s32[1,1280]{1,0:T(1,128)} %reshape.26.m_ref) | copy-start | bytes 15364
  42.2 9.1 %copy-start.5 = (bf16[5,2,1408,256]{3,2,1,0:T(8,128)(2,1)S(1)}, bf16[5,2,1408,256]{3,2,1,0:T(8,128)(2,1)}, u32[]{:S(2)}) copy-start(bf16[5,2,1408,256]{3,2,1,0:T(8,128)(2,1)} %get-tuple-element.12.table) | copy-start | bytes 21626884
  42.2 9.1 %copy-start.7 = (f32[2]{0:T(128)S(1)}, f32[2]{0:T(128)}, u32[]{:S(2)}) copy-start(f32[2]{0:T(128)} %weight_ref.1) | copy-start | bytes 28
  50.2 20.3 %collective-permute-start = (bf16[3,336,384]{2,1,0:T(8,128)(2,1)S(1)}, bf16[3,336,384]{2,1,0:T(8,128)(2,1)S(1)}, u32[]{:S(2)}, u32[]{:S(2)}) collective-permute-start(bf16[3,336,384]{2,1,0:T(8,128)(2,1)S(1)} %get-tuple-element.17), channel_id=1, source_target_pairs={{0,1},{1,0},{2,3},{3,2},{4,5},{5,4},{6,7},{7,6},{8,9},{9,8},{10,11... | collective-permute-start | bytes 2322440 | tf_op jit(solution)/shard_map/ppermute | solution.py:625
  57.9 22.3 %all-to-all-start.1 = ((bf16[128,24,128]{2,1,0:T(8,128)(2,1)}), bf16[128,24,128]{2,1,0:T(8,128)(2,1)S(1)}, u32[]{:S(2)}, u32[]{:S(2)}) async-start(bf16[128,24,128]{2,1,0:T(8,128)(2,1)} %bitcast.4), calls=%async_computation.1 | async-start | bytes 1572864 | tf_op jit(solution)/shard_map/all_to_all | solution.py:627
  70.8 9.4 %copy-start.2 = (s32[800]{0:T(1024)S(1)}, s32[800]{0:T(1024)}, u32[]{:S(2)}) copy-start(s32[800]{0:T(1024)} %get-tuple-element.10.order_ref) | copy-start | bytes 9604
  70.8 9.4 %copy-start.3 = (s32[21]{0:T(128)S(1)}, s32[21]{0:T(128)}, u32[]{:S(2)}) copy-start(s32[21]{0:T(128)} %get-tuple-element.11.count_ref) | copy-start | bytes 256

commit v4 on v3

--- a/solution.py
+++ b/solution.py
@@ -22,6 +22,7 @@
 OUTR = 336
 GROUP = 16
 RUNS = ((0, 32), (32, 96), (128, 96), (224, 96), (320, 80))
+ARRIVALS = ((0, 16), (16, 64), (80, 96), (176, 112), (288, 112))
 STRIDE = 73
 FEW = 5
 
@@ -42,7 +43,7 @@
 
 def copy_in(spec_hbm, leg_hbm, spec, leg, sems):
     copies = []
-    for n, (first, count) in enumerate(RUNS):
+    for n, (first, count) in enumerate(ARRIVALS):
         pair = [
             pltpu.make_async_copy(
                 leg_hbm.at[pl.ds(first, count)], leg.at[pl.ds(first, count)], sems.at[0, n]
@@ -96,7 +97,7 @@
             order_ref[slot * 20 + seen] = base + kk
         return carry
 
-    for (first, count), pair in zip(RUNS, copies):
+    for (first, count), pair in zip(ARRIVALS, copies):
         for copy in pair:
             copy.wait()
         lax.fori_loop(first // GROUP, (first + count) // GROUP, body, 0, unroll=True)
@@ -128,7 +129,7 @@
         scratch_shapes=[
             pltpu.VMEM(spec.shape, bf16),
             pltpu.VMEM(legendre.shape, bf16),
-            pltpu.SemaphoreType.DMA((2, len(RUNS))),
+            pltpu.SemaphoreType.DMA((2, len(ARRIVALS))),
             pltpu.VMEM((SLOTS + 1, 144, 128), f32),
             pltpu.VMEM((GROUP * 80, 128), f32),
             pltpu.VMEM((ROWS * 128, 128), f32),
@@ -566,7 +567,7 @@
             pltpu.VMEM((128 * ROWS, 128), f32),
         ],
         compiler_params=params(16),
-        cost_estimate=pl.CostEstimate(flops=1 << 33, bytes_accessed=1 << 20, transcendentals=0),
+        cost_estimate=pl.CostEstimate(flops=1 << 34, bytes_accessed=1 << 20, transcendentals=0),
         name="unpack",
     )(payload, m_row)
 

time: 91.8 us -> 91.6 us (level)
  no operation moved by 1% of the time
where the time goes in v4:
time: 91.6 us; the launch traced here: 91.1 us
  Pallas kernels  52.2 us (57%)
  starting transfers between devices  17.8 us (19%)
  waiting for transfers between devices  13.5 us (15%)
  local copies, waits for them, and re-layouts  6.4 us (7%)
  between operations  0.94 us (1%)
    all_to_all x1, starting transfers between devices, local(): lax.all_to_all(sent, ('wave', 'lev'), split_axis=0, concat_axis=0, tiled=...  11.5 us
    pallas_call x1, Pallas kernels, analysis(): pl.pallas_call(analysis_kernel, in_specs=[pl.BlockSpec(memory_space=pltpu...  11 us
    pallas_call x1, Pallas kernels, synthesis(): pl.pallas_call(synthesis_kernel, in_specs=[pl.BlockSpec(memory_space=pltp...  9.42 us
    pallas_call x1, Pallas kernels, tables(): pl.pallas_call(table_kernel, in_specs=[pl.BlockSpec(memory_space=pltpu.SM...  9.22 us
    pallas_call x1, Pallas kernels, inverse(): pl.pallas_call(inverse_kernel, in_specs=[pl.BlockSpec(memory_space=pltpu....  7.96 us
    pallas_call x1, Pallas kernels, arrange(): pl.pallas_call(arrange_kernel, in_specs=[smem, smem, pl.BlockSpec(memory_...  6.81 us
    pallas_call x1, Pallas kernels, forward(): pl.pallas_call(forward_kernel, in_specs=[pl.BlockSpec(memory_space=pltpu....  6.54 us
    all_to_all x1, waiting for transfers between devices, local(): lax.all_to_all(sent, ('wave', 'lev'), split_axis=0, concat_axis=0, tiled=...  6.53 us
  transfers between devices with their start and end apart: 3, of which 3 were waited for; matrix products, arithmetic and copies ran while one was open for 5% of the time, Pallas kernels for 25%

profile of v4, /device:TPU:1, one launch (start us, length us, event | category | flops | bytes accessed | tf_op | source)
XLA Modules:
  0.0 91.1 jit_solution(15985762765951370007)
XLA Ops:
  0.6 0.0 copy-start.8
  0.6 9.4 %synthesis.1 = (bf16[3072,128]{1,0:T(8,128)(2,1)}, s32[800]{0:T(1024)}, s32[21]{0:T(128)}) custom-call(s32[400]{0:T(512)} %slot_ref.1, bf16[6,400,1536]{2,1,0:T(8,128)(2,1)} %bitcast.16, bf16[400,64,128]{2,1,0:T(8,128)(2,1)} %leg_hbm.3), custom_call_target="tpu_custom_call" | custom-call | tf_op jit(solution)/shard_map/synthesis/pallas_call | solution.py:117
  10.1 11.5 %all-to-all-start = ((bf16[128,24,128]{2,1,0:T(8,128)(2,1)}), bf16[128,24,128]{2,1,0:T(8,128)(2,1)S(1)}, u32[]{:S(2)}, u32[]{:S(2)}) async-start(bf16[128,24,128]{2,1,0:T(8,128)(2,1)} %bitcast.17), calls=%async_computation | async-start | bytes 1572864 | tf_op jit(solution)/shard_map/all_to_all | solution.py:621
  21.6 0.0 copy-done.8
  21.6 0.1 reshape.25
  21.7 0.1 copy.9
  21.8 0.7 reshape.26.m_ref
  22.5 9.2 %tables.1 = (bf16[5,2,1408,256]{3,2,1,0:T(8,128)(2,1)}, bf16[2560,1408]{1,0:T(8,128)(2,1)}) custom-call(s32[2]{0:T(128)} %points_ref.3, s32[1,1280]{1,0:T(1,128)} %reshape.26.m_ref), custom_call_target="tpu_custom_call" | custom-call | tf_op jit(solution)/shard_map/tables/pallas_call | solution.py:390
  31.7 6.5 %all-to-all-done = bf16[128,24,128]{2,1,0:T(8,128)(2,1)S(1)} async-done(((bf16[128,24,128]{2,1,0:T(8,128)(2,1)}), bf16[128,24,128]{2,1,0:T(8,128)(2,1)S(1)}, u32[]{:S(2)}, u32[]{:S(2)}) %all-to-all-start) | async-done | bytes 786464 | tf_op jit(solution)/shard_map/all_to_all | solution.py:621
  38.2 0.7 copy-done
  38.9 1.2 %unpack.1.coef = bf16[576,2560]{1,0:T(8,128)(2,1)S(1)} custom-call(bf16[3072,128]{1,0:T(8,128)(2,1)S(1)} %bitcast.14, s32[1,1280]{1,0:T(1,128)S(1)} %copy-done), custom_call_target="tpu_custom_call" | custom-call | flops 17179869184 | bytes 1048576 | tf_op jit(solution)/shard_map/unpack/pallas_call | solution.py:560
  40.2 0.0 copy-done.4
  40.2 1.8 %copy-done.6 = bf16[2560,1408]{1,0:T(8,128)(2,1)S(1)} copy-done((bf16[2560,1408]{1,0:T(8,128)(2,1)S(1)}, bf16[2560,1408]{1,0:T(8,128)(2,1)}, u32[]{:S(2)}) %copy-start.6) | copy-done | bytes 7208984
  42.0 8.0 %inverse.1 = (bf16[576,1408]{1,0:T(8,128)(2,1)S(1)}, bf16[3,336,384]{2,1,0:T(8,128)(2,1)S(1)}, bf16[3,336,384]{2,1,0:T(8,128)(2,1)S(1)}) custom-call(s32[2]{0:T(128)S(1)} %copy-done.4, bf16[576,2560]{1,0:T(8,128)(2,1)S(1)} %unpack.1.coef, bf16[2560,1408]{1,0:T(8,128)(2,1)S(1)} %copy-done.6), custom_call_target="tpu_custom_call" | custom-call | flops 4152360960 | bytes 12582912 | tf_op jit(solution)/shard_map/inverse/pallas_call | solution.py:577
  50.0 1.1 %collective-permute-start = (bf16[3,336,384]{2,1,0:T(8,128)(2,1)S(1)}, bf16[3,336,384]{2,1,0:T(8,128)(2,1)S(1)}, u32[]{:S(2)}, u32[]{:S(2)}) collective-permute-start(bf16[3,336,384]{2,1,0:T(8,128)(2,1)S(1)} %get-tuple-element.17), channel_id=1, source_target_pairs={{0,1},{1,0},{2,3},{3,2},{4,5},{5,4},{6,7},{7,6},{8,9},{9,8},{10,11... | collective-permute-start | bytes 2322440 | tf_op jit(solution)/shard_map/ppermute | solution.py:626
  51.1 0.0 copy-done.1
  51.1 0.0 copy-done.5
  51.1 0.0 copy-done.7
  51.1 6.5 %forward.1 = bf16[3072,128]{1,0:T(8,128)(2,1)} custom-call(f32[2]{0:T(128)S(1)} %copy-done.7, s32[1,1280]{1,0:T(1,128)S(1)} %copy-done.1, bf16[5,2,1408,256]{3,2,1,0:T(8,128)(2,1)S(1)} %copy-done.5, bf16[576,1408]{1,0:T(8,128)(2,1)S(1)} %get-tuple-element.15.flux), custom_call_target="tpu_custom_call" | custom-call | flops 4152360960 | bytes 12582912 | tf_op jit(solution)/shard_map/forward/pallas_call | solution.py:597
  57.6 5.2 %all-to-all-start.1 = ((bf16[128,24,128]{2,1,0:T(8,128)(2,1)}), bf16[128,24,128]{2,1,0:T(8,128)(2,1)S(1)}, u32[]{:S(2)}, u32[]{:S(2)}) async-start(bf16[128,24,128]{2,1,0:T(8,128)(2,1)} %bitcast.4), calls=%async_computation.1 | async-start | bytes 1572864 | tf_op jit(solution)/shard_map/all_to_all | solution.py:628
  62.8 6.8 %arrange.1.leg_hbm = bf16[100,128,256]{2,1,0:T(8,128)(2,1)} custom-call(s32[800]{0:T(1024)} %get-tuple-element.10.order_ref, s32[21]{0:T(128)} %get-tuple-element.11.count_ref, bf16[400,64,128]{2,1,0:T(8,128)(2,1)} %leg_hbm.3), custom_call_target="tpu_custom_call" | custom-call | flops 4294967296 | bytes 14680064 | tf_op jit(solution)/shard_map/arrange/pallas_call | solution.py:182
  69.6 0.7 collective-permute-done
  70.2 0.1 select_bitcast_fusion.1
  70.4 0.2 pad_maximum_fusion
  70.6 0.0 copy-start.2
  70.6 0.0 copy-start.3
  70.6 0.2 copy.10
  70.7 2.9 %reshape.31 = bf16[2,3,123264]{2,0,1:T(2,128)(2,1)} reshape(bf16[2,3,321,384]{3,2,0,1:T(8,128)(2,1)S(1)} %copy.10) | data formatting | bytes 2958336 | tf_op jit(solution)/shard_map/reshape | solution.py:639
  73.6 6.3 %all-to-all-done.1 = bf16[128,24,128]{2,1,0:T(8,128)(2,1)S(1)} async-done(((bf16[128,24,128]{2,1,0:T(8,128)(2,1)}), bf16[128,24,128]{2,1,0:T(8,128)(2,1)S(1)}, u32[]{:S(2)}, u32[]{:S(2)}) %all-to-all-start.1) | async-done | bytes 786464 | tf_op jit(solution)/shard_map/all_to_all | solution.py:628
  79.9 0.0 copy-done.2
  79.9 0.0 copy-done.3
  79.9 11.0 %analysis.1 = bf16[6,400,1536]{2,1,0:T(8,128)(2,1)} custom-call(s32[800]{0:T(1024)S(1)} %copy-done.2, s32[21]{0:T(128)S(1)} %copy-done.3, bf16[3072,128]{1,0:T(8,128)(2,1)S(1)} %bitcast.13, bf16[100,128,256]{2,1,0:T(8,128)(2,1)} %arrange.1.leg_hbm), custom_call_target="tpu_custom_call" | custom-call | tf_op jit(solution)/shard_map/analysis/pallas_call | solution.py:270
  (6 shorter events, 0.0 us)
Async XLA Ops:
  0.6 21.0 %copy-start.8 = (s32[1280]{0:T(1024)S(1)}, s32[1280]{0:T(1024)}, u32[]{:S(2)}) copy-start(s32[1280]{0:T(1024)} %param.9) | copy-start | bytes 15364
  10.1 28.2 %all-to-all-start = ((bf16[128,24,128]{2,1,0:T(8,128)(2,1)}), bf16[128,24,128]{2,1,0:T(8,128)(2,1)S(1)}, u32[]{:S(2)}, u32[]{:S(2)}) async-start(bf16[128,24,128]{2,1,0:T(8,128)(2,1)} %bitcast.17), calls=%async_computation | async-start | bytes 1572864 | tf_op jit(solution)/shard_map/all_to_all | solution.py:621
  38.2 0.7 copy-start
  38.9 1.2 %copy-start.4 = (s32[2]{0:T(128)S(1)}, s32[2]{0:T(128)}, u32[]{:S(2)}) copy-start(s32[2]{0:T(128)} %points_ref.3) | copy-start | bytes 28
  38.9 3.1 %copy-start.6 = (bf16[2560,1408]{1,0:T(8,128)(2,1)S(1)}, bf16[2560,1408]{1,0:T(8,128)(2,1)}, u32[]{:S(2)}) copy-start(bf16[2560,1408]{1,0:T(8,128)(2,1)} %get-tuple-element.14.flip) | copy-start | bytes 21626884
  42.0 9.1 %copy-start.1 = (s32[1,1280]{1,0:T(1,128)S(1)}, s32[1,1280]{1,0:T(1,128)}, u32[]{:S(2)}) copy-start(s32[1,1280]{1,0:T(1,128)} %reshape.26.m_ref) | copy-start | bytes 15364
  42.0 9.1 %copy-start.5 = (bf16[5,2,1408,256]{3,2,1,0:T(8,128)(2,1)S(1)}, bf16[5,2,1408,256]{3,2,1,0:T(8,128)(2,1)}, u32[]{:S(2)}) copy-start(bf16[5,2,1408,256]{3,2,1,0:T(8,128)(2,1)} %get-tuple-element.12.table) | copy-start | bytes 21626884
  42.0 9.1 %copy-start.7 = (f32[2]{0:T(128)S(1)}, f32[2]{0:T(128)}, u32[]{:S(2)}) copy-start(f32[2]{0:T(128)} %weight_ref.1) | copy-start | bytes 28
  50.0 20.3 %collective-permute-start = (bf16[3,336,384]{2,1,0:T(8,128)(2,1)S(1)}, bf16[3,336,384]{2,1,0:T(8,128)(2,1)S(1)}, u32[]{:S(2)}, u32[]{:S(2)}) collective-permute-start(bf16[3,336,384]{2,1,0:T(8,128)(2,1)S(1)} %get-tuple-element.17), channel_id=1, source_target_pairs={{0,1},{1,0},{2,3},{3,2},{4,5},{5,4},{6,7},{7,6},{8,9},{9,8},{10,11... | collective-permute-start | bytes 2322440 | tf_op jit(solution)/shard_map/ppermute | solution.py:626
  57.6 22.3 %all-to-all-start.1 = ((bf16[128,24,128]{2,1,0:T(8,128)(2,1)}), bf16[128,24,128]{2,1,0:T(8,128)(2,1)S(1)}, u32[]{:S(2)}, u32[]{:S(2)}) async-start(bf16[128,24,128]{2,1,0:T(8,128)(2,1)} %bitcast.4), calls=%async_computation.1 | async-start | bytes 1572864 | tf_op jit(solution)/shard_map/all_to_all | solution.py:628
  70.6 9.4 %copy-start.2 = (s32[800]{0:T(1024)S(1)}, s32[800]{0:T(1024)}, u32[]{:S(2)}) copy-start(s32[800]{0:T(1024)} %get-tuple-element.10.order_ref) | copy-start | bytes 9604
  70.6 9.4 %copy-start.3 = (s32[21]{0:T(128)S(1)}, s32[21]{0:T(128)}, u32[]{:S(2)}) copy-start(s32[21]{0:T(128)} %get-tuple-element.11.count_ref) | copy-start | bytes 256
